TPU v7x, 768 devices: a whole 4x8x12 slice. The times are simulated.
768 devices in a mesh: span: 32 (over x, z_hi, core), chord: 24 (over y, z_lo).
Axes of the slice: x: 4, y: 8, z: 12 (z_hi: 4, z_lo: 3; z = z_hi * 3 + z_lo), core: 2. Of those that a mesh axis runs over, the one named last changes fastest.
Arguments:
- traces: float32 [2, 45, 589824], P(None, None, ('span', 'chord')), may hold values from -6 to 6
- source: float32 [2, 135, 196608], P(None, None, ('span', 'chord')), may hold values from -6 to 6
- scales: float32 [135, 6144], P(None, ('span', 'chord')), may hold values from 0.5 to 2
- inverse_local: float32 [2, 135, 135], replicated, may hold values from -0.375 to 0.375
- lift_map: float32 [2, 135, 270], replicated, may hold values from -0.25 to 0.25
- trace_map: float32 [2, 270, 135], replicated, may hold values from -0.375 to 0.375
- stabilizer: float32 [2, 270, 270], replicated, may hold values from -0.25 to 0.25
- elem_faces: int32 [6144, 6], P(('span', 'chord')), may hold values from 0 to 39, as said below
- send_faces: int32 [32, 24, 4, 4], P('span', 'chord'), may hold values from 0 to 23, as said below
- counts: int32 [32, 24], P('span', 'chord'), may hold values from 4 to 8, as said below
Outputs:
- interior_field: float32 [2, 135, 196608], P(None, None, ('span', 'chord'))
- residual: float32 [2, 45, 589824], P(None, None, ('span', 'chord'))
Inputs may be any that keep to these rules, and one draw needn't show every extreme that they name: `elem_faces`: in a partition, entries of element slots 4 and later are below 24; every ghost number is referenced exactly once. `send_faces`: the 4 entries of one partition and direction are distinct. `counts`: some partition is full.
All inputs are finite; a program needn't handle non-finite values.
Results may differ from a plain program's by a relative error of at most 0.0003.
Values sent between devices are 32-bit elements; how exact they have to be, the bound alone decides.
No kernel may reach another device: no remote copies, remote signals or barrier semaphores. Data moves between devices by JAX's collectives and lax.ppermute only.
A program may use at most 32 MiB of HBM per device.

v0:
```python
import math

import jax
import jax.numpy as jnp
from jax import lax
from jax.sharding import PartitionSpec as P

ANG = 32


def padded(block, sides, width, periodic):
    for axis, dim in sides:
        count = lax.axis_size(axis)
        forward = [(i, i + 1) for i in range(count - 1)]
        if periodic:
            forward.append((count - 1, 0))
        backward = [(target, source) for source, target in forward]
        low = lax.ppermute(
            lax.slice_in_dim(block, block.shape[dim] - width, None, axis=dim), axis, forward
        )
        high = lax.ppermute(lax.slice_in_dim(block, 0, width, axis=dim), axis, backward)
        block = jnp.concatenate([low, block, high], axis=dim)
    return block


def exact_dot(left, right):
    return jnp.dot(left, right, precision=lax.Precision.HIGHEST, preferred_element_type=jnp.float32)


def complex_block(matrix):
    top = jnp.concatenate([matrix[0], -matrix[1]], axis=1)
    bottom = jnp.concatenate([matrix[1], matrix[0]], axis=1)
    return jnp.concatenate([top, bottom], axis=0)


def element_terms(face_table, faces, source_cols, scale_cols, live_mask, operators):
    block_inv, block_lift, block_trace, block_stab = operators
    amount = faces.shape[0]
    face_dof = face_table.shape[1]
    angles = face_table.shape[3]
    cell_dof = scale_cols.shape[0]
    face_index = faces.T
    gathered = face_table[:, :, face_index, :]
    trace_cols = jnp.transpose(gathered, (0, 2, 1, 3, 4)).reshape(12 * face_dof, amount * angles)
    interior_rhs = source_cols.reshape(2 * cell_dof, amount * angles) - exact_dot(
        block_lift, trace_cols
    )
    interior_rhs = (
        interior_rhs.reshape(2, cell_dof, amount, angles) * scale_cols[None, :, :, None]
    ).reshape(2 * cell_dof, amount * angles)
    interior = (
        exact_dot(block_inv, interior_rhs).reshape(2, cell_dof, amount, angles)
        * live_mask[None, None, :, None]
    )
    face_terms = exact_dot(
        block_trace, interior.reshape(2 * cell_dof, amount * angles)
    ) + exact_dot(block_stab, trace_cols)
    face_terms = (
        face_terms.reshape(2, 6, face_dof, amount, angles) * live_mask[None, None, None, :, None]
    )
    face_terms = jnp.transpose(face_terms, (0, 2, 1, 3, 4))
    face_sums = jnp.zeros(face_table.shape, jnp.float32).at[:, :, face_index, :].add(face_terms)
    return (interior.reshape(2, cell_dof, amount * angles), face_sums)


def run_range(face_table, elem_faces, source, scales, live_total, operators):
    return element_terms(face_table, elem_faces, source, scales, live_total, operators)


def local(
    traces,
    source,
    scales,
    inverse_local,
    lift_map,
    trace_map,
    stabilizer,
    elem_faces,
    send_faces,
    counts,
):
    face_dof = traces.shape[1]
    own_faces = traces.shape[2] // ANG
    slots_all = elem_faces.shape[0]
    per_side = send_faces.shape[3]
    own_table = traces.reshape(2, face_dof, own_faces, ANG)
    send_lists = send_faces.reshape(4, per_side)
    live_count = counts.reshape(())
    live_total = (jnp.arange(slots_all) < live_count).astype(jnp.float32)
    operators = (
        complex_block(inverse_local),
        complex_block(lift_map),
        complex_block(trace_map),
        complex_block(stabilizer),
    )
    phases = 2.0 * math.pi * jnp.arange(ANG).astype(jnp.float32) / ANG
    span_place = lax.axis_index("span")
    span_length = lax.axis_size("span")
    lower_sign = jnp.where(span_place == 0, -1.0, 0.0).astype(jnp.float32)
    upper_sign = jnp.where(span_place == span_length - 1, 1.0, 0.0).astype(jnp.float32)

    def rotate(values, turn_sign):
        cosine = jnp.cos(turn_sign * phases)
        sine_part = jnp.sin(turn_sign * phases)
        return jnp.stack(
            [values[0] * cosine - values[1] * sine_part, values[0] * sine_part + values[1] * cosine]
        )

    outgoing = own_table[:, :, send_lists, :]
    chord_out = jnp.stack([outgoing[:, :, 0], outgoing[:, :, 1]])
    span_out = jnp.stack([outgoing[:, :, 2], outgoing[:, :, 3]])
    chord_in = padded(chord_out, (("chord", 0),), 1, False)
    span_in = padded(span_out, (("span", 0),), 1, True)
    face_table = jnp.concatenate(
        [
            own_table,
            chord_in[0],
            chord_in[3],
            rotate(span_in[0], lower_sign),
            rotate(span_in[3], upper_sign),
        ],
        axis=2,
    )
    interior, face_sums = run_range(face_table, elem_faces, source, scales, live_total, operators)
    borrowed = [
        face_sums[:, :, own_faces + side * per_side : own_faces + (side + 1) * per_side]
        for side in range(4)
    ]
    chord_back = padded(jnp.stack([borrowed[0], borrowed[1]]), (("chord", 0),), 1, False)
    span_back = padded(
        jnp.stack([rotate(borrowed[2], -lower_sign), rotate(borrowed[3], -upper_sign)]),
        (("span", 0),),
        1,
        True,
    )
    residual = face_sums[:, :, :own_faces]
    residual = residual.at[:, :, send_lists[0]].add(chord_back[0])
    residual = residual.at[:, :, send_lists[1]].add(chord_back[3])
    residual = residual.at[:, :, send_lists[2]].add(span_back[0])
    residual = residual.at[:, :, send_lists[3]].add(span_back[3])
    return (interior, residual.reshape(2, face_dof, own_faces * ANG))


def solution(mesh):
    in_specs = (
        P(None, None, ("span", "chord")),
        P(None, None, ("span", "chord")),
        P(None, ("span", "chord")),
        P(),
        P(),
        P(),
        P(),
        P(("span", "chord"), None),
        P("span", "chord", None, None),
        P("span", "chord"),
    )
    out_specs = (P(None, None, ("span", "chord")), P(None, None, ("span", "chord")))
    return jax.shard_map(local, mesh=mesh, in_specs=in_specs, out_specs=out_specs, check_vma=False)
```

profile of v0, /device:TPU:152, one launch (start us, length us, event | category | flops | bytes accessed | tf_op | source)
XLA Modules:
  0.0 86.0 jit_solution(4825053477813422030)
XLA Ops:
  2.3 1.2 %copy.82 = f32[2,45,768]{1,2,0:T(8,128)S(1)} copy(f32[2,45,768]{2,0,1:T(2,128)} %param.10) | data formatting | bytes 552960 | tf_op jit(solution)/shard_map/reshape | solution.py:86
  4.2 0.8 slice_bitcast_fusion.2
  5.0 2.9 %collective-permute-start = (f32[1,2,45,4,32]{2,4,3,1,0:T(8,128)}, f32[1,2,45,4,32]{2,4,3,1,0:T(8,128)}, u32[]{:S(2)}, u32[]{:S(2)}) collective-permute-start(f32[1,2,45,4,32]{2,4,3,1,0:T(8,128)} %get-tuple-element.21), channel_id=1, source_target_pairs={{0,1},{1,2},{2,3},{3,4},{4,5},{5,6},{6,7},{7,8},{8,9},{9,10},{10,1... | collective-permute-start | bytes 138248 | tf_op jit(solution)/shard_map/ppermute | solution.py:18
  7.9 3.0 %collective-permute-start.1 = (f32[1,2,45,4,32]{2,4,3,1,0:T(8,128)}, f32[1,2,45,4,32]{2,4,3,1,0:T(8,128)}, u32[]{:S(2)}, u32[]{:S(2)}) collective-permute-start(f32[1,2,45,4,32]{2,4,3,1,0:T(8,128)} %get-tuple-element.20), channel_id=1, source_target_pairs={{1,0},{2,1},{3,2},{4,3},{5,4},{6,5},{7,6},{8,7},{9,8},{10,9},{11,1... | collective-permute-start | bytes 138248 | tf_op jit(solution)/shard_map/ppermute | solution.py:21
  10.8 1.9 %collective-permute-start.2 = (f32[1,2,45,4,32]{2,4,3,1,0:T(8,128)}, f32[1,2,45,4,32]{2,4,3,1,0:T(8,128)}, u32[]{:S(2)}, u32[]{:S(2)}) collective-permute-start(f32[1,2,45,4,32]{2,4,3,1,0:T(8,128)} %get-tuple-element.19), channel_id=1, source_target_pairs={{0,24},{24,48},{48,72},{72,96},{96,120},{120,144},{144,168},{168,1... | collective-permute-start | bytes 138248 | tf_op jit(solution)/shard_map/ppermute | solution.py:18
  12.8 14.9 %collective-permute-start.3 = (f32[1,2,45,4,32]{2,4,3,1,0:T(8,128)}, f32[1,2,45,4,32]{2,4,3,1,0:T(8,128)}, u32[]{:S(2)}, u32[]{:S(2)}) collective-permute-start(f32[1,2,45,4,32]{2,4,3,1,0:T(8,128)} %get-tuple-element.18), channel_id=1, source_target_pairs={{24,0},{48,24},{72,48},{96,72},{120,96},{144,120},{168,144},{192,1... | collective-permute-start | bytes 138248 | tf_op jit(solution)/shard_map/ppermute | solution.py:21
  28.9 0.8 copy_bitcast_fusion.6
  31.3 0.8 fusion.43
  32.0 1.0 %copy_bitcast_fusion.2 = (f32[270,270]{1,0:T(8,128)}, f32[270,270]{1,0:T(8,128)}) fusion(f32[1,270,270]{2,0,1:T(1,128)S(1)} %get-tuple-element.16, f32[1,270,270]{2,0,1:T(1,128)S(1)} %get-tuple-element.17), kind=kLoop, calls=%fused_computation.38 | loop fusion | bytes 1166400 | tf_op jit(solution)/shard_map/squeeze | solution.py:31
  34.1 0.8 copy_bitcast_fusion.4
  36.0 0.8 reshape.396
  36.8 0.9 %bitcast_dynamic-update-slice_fusion.1 = f32[2,45,40,32]{1,3,2,0:T(8,128)S(1)} fusion(f32[2,45,40,32]{1,3,2,0:T(8,128)S(1)} %constant_dynamic-update-slice_fusion, f32[1,2,45,4,32]{2,4,3,1,0:T(8,128)} %collective-permute-done), kind=kLoop, calls=%fused_computation.58 | loop fusion | bytes 177152
  37.7 0.9 %bitcast_dynamic-update-slice_fusion = f32[2,45,40,32]{1,3,2,0:T(8,128)S(1)} fusion(f32[2,45,40,32]{1,3,2,0:T(8,128)S(1)} %bitcast_dynamic-update-slice_fusion.1, f32[1,2,45,4,32]{2,4,3,1,0:T(8,128)} %collective-permute-done.1), kind=kLoop, calls=%fused_computation.57 | loop fusion | bytes 177152
  38.6 1.0 %multiply_subtract_fusion.3 = (f32[1,45,4,32]{1,3,2,0:T(8,128)S(1)}, f32[1,45,4,32]{1,3,2,0:T(8,128)S(1)}) fusion(f32[1,2,45,4,32]{2,4,3,1,0:T(8,128)} %collective-permute-done.2, f32[32]{0:T(128)S(1)} %get-tuple-element.38, f32[32]{0:T(128)S(1)} %get-tuple-element.39), kind=kLoop, calls=%fused_computation.70 | loop fusion | flops 34560 | bytes 92416 | tf_op jit(solution)/shard_map/sub | solution.py:106
  39.6 1.0 %multiply_subtract_fusion.2 = (f32[1,45,4,32]{1,3,2,0:T(8,128)S(1)}, f32[1,45,4,32]{1,3,2,0:T(8,128)S(1)}) fusion(f32[1,2,45,4,32]{2,4,3,1,0:T(8,128)} %collective-permute-done.3, f32[32]{0:T(128)S(1)} %get-tuple-element.40, f32[32]{0:T(128)S(1)} %get-tuple-element.41), kind=kLoop, calls=%fused_computation.68 | loop fusion | flops 34560 | bytes 92416 | tf_op jit(solution)/shard_map/sub | solution.py:106
  41.3 2.2 %copy.109 = f32[6,8,2,45,32]{3,0,2,4,1:T(8,128)} copy(f32[6,8,2,45,32]{3,4,2,1,0:T(8,128)S(1)} %bitcast.138) | data formatting | bytes 1105920 | tf_op jit(solution)/shard_map/gather | solution.py:43
  43.5 2.3 %reshape.329 = f32[540,256]{0,1:T(8,128)S(1)} reshape(f32[2,6,45,8,32]{2,1,0,4,3:T(8,128)} %bitcast.140) | data formatting | bytes 1105920 | tf_op jit(solution)/shard_map/reshape | solution.py:44
  45.9 0.9 %fusion.9 = f32[256,270]{0,1:T(8,128)S(1)} fusion(f32[270,256]{1,0:T(8,128)S(1)} %copy.66, f32[270,256]{1,0:T(8,128)S(1)} %reshape.326, f32[540,256]{0,1:T(8,128)S(1)} %reshape.329, f32[135,270]{1,0:T(8,128)S(1)} %copy-done.2, f32[135,270]{1,0:T(8,128)S(1)} %copy-done.1, f32[135,270]{1,0:T(8,128)S(1)} %copy-done.5), kind=kOutput, calls=%fused_computation.21 | convolution fusion | flops 448473248 | bytes 1819800 | tf_op jit(solution)/shard_map/dot_general | solution.py:27
  47.0 1.0 %convolution_multiply_fusion = f32[2,135,8,32]{1,3,2,0:T(8,128)S(1)} fusion(f32[8,32,270,1]{2,1,0,3:T(8,128)S(1)} %bitcast.147, f32[2,135,270,1]{2,1,0,3:T(8,128)S(1)} %copy-done, f32[8]{0:T(128)S(1)} %compare_convert_fusion), kind=kOutput, calls=%fused_computation.18 | convolution fusion | flops 224017920 | bytes 844592 | tf_op jit(solution)/shard_map/dot_general | solution.py:27
  48.9 2.9 %fusion = f32[540,256]{1,0:T(8,128)S(1)} fusion(f32[540,256]{0,1:T(8,128)S(1)} %reshape.329, f32[270,270]{1,0:T(8,128)} %get-tuple-element.47, f32[270,270]{1,0:T(8,128)S(1)} %copy-done.8, f32[270,270]{1,0:T(8,128)} %fusion.43), kind=kOutput, calls=%fused_computation.9 | convolution fusion | flops 896670016 | bytes 1980720 | tf_op jit(solution)/shard_map/dot_general | solution.py:27
  51.9 1.8 %convolution_add_fusion = f32[540,256]{1,0:T(8,128)S(1)} fusion(f32[540,256]{1,0:T(8,128)S(1)} %fusion, f32[270,256]{0,1:T(8,128)S(1)} %reshape.332, f32[270,135]{0,1:T(8,128)S(1)} %copy-done.4, f32[270,135]{0,1:T(8,128)S(1)} %copy-done.3, f32[270,135]{0,1:T(8,128)S(1)} %copy-done.6), kind=kOutput, calls=%fused_computation.17 | convolution fusion | flops 448473248 | bytes 1819800 | tf_op jit(solution)/shard_map/dot_general | solution.py:27
  53.9 1.2 %reshape.333 = f32[2,6,45,8,32]{2,1,0,4,3:T(8,128)S(1)} reshape(f32[540,256]{0,1:T(8,128)S(1)} %copy.73) | data formatting | bytes 1105920 | tf_op jit(solution)/shard_map/reshape | solution.py:59
  56.0 3.5 %scatter_fusion = f32[2,45,40,32]{1,3,2,0:T(8,128)S(1)} fusion(f32[2,45,40,32]{1,3,2,0:T(8,128)S(1)} %broadcast_in_dim.5, s32[48]{0:T(128)S(1)} %reshape.345, f32[48,2,45,32]{2,3,1,0:T(8,128)S(1)} %bitcast.139), kind=kCustom, calls=%fused_computation.2 | custom fusion | flops 138240 | bytes 1659072 | tf_op jit(solution)/shard_map/scatter-add | solution.py:62
  60.4 2.9 %collective-permute-start.7 = (f32[1,2,45,4,32]{2,4,3,1,0:T(8,128)S(1)}, f32[1,2,45,4,32]{2,4,3,1,0:T(8,128)S(1)}, u32[]{:S(2)}, u32[]{:S(2)}) collective-permute-start(f32[1,2,45,4,32]{2,4,3,1,0:T(8,128)S(1)} %maximum_bitcast_fusion.1), channel_id=1, source_target_pairs={{24,0},{48,24},{72,48},{96,72},{120,96},{144,120},{168,144},{192,1... | collective-permute-start | bytes 138248 | tf_op jit(solution)/shard_map/ppermute | solution.py:21
  63.2 1.9 %collective-permute-start.6 = (f32[1,2,45,4,32]{2,4,3,1,0:T(8,128)S(1)}, f32[1,2,45,4,32]{2,4,3,1,0:T(8,128)S(1)}, u32[]{:S(2)}, u32[]{:S(2)}) collective-permute-start(f32[1,2,45,4,32]{2,4,3,1,0:T(8,128)S(1)} %maximum_bitcast_fusion), channel_id=1, source_target_pairs={{0,24},{24,48},{48,72},{72,96},{96,120},{120,144},{144,168},{168,1... | collective-permute-start | bytes 138248 | tf_op jit(solution)/shard_map/ppermute | solution.py:18
  65.2 6.9 %collective-permute-start.4 = (f32[1,2,45,4,32]{2,4,3,1,0:T(8,128)}, f32[1,2,45,4,32]{2,4,3,1,0:T(8,128)S(1)}, u32[]{:S(2)}, u32[]{:S(2)}) collective-permute-start(f32[1,2,45,4,32]{2,4,3,1,0:T(8,128)} %get-tuple-element.15), channel_id=1, source_target_pairs={{0,1},{1,2},{2,3},{3,4},{4,5},{5,6},{6,7},{7,8},{8,9},{9,10},{10,1... | collective-permute-start | bytes 138248 | tf_op jit(solution)/shard_map/ppermute | solution.py:18
  72.1 1.9 %collective-permute-start.5 = (f32[1,2,45,4,32]{2,4,3,1,0:T(8,128)S(1)}, f32[1,2,45,4,32]{2,4,3,1,0:T(8,128)S(1)}, u32[]{:S(2)}, u32[]{:S(2)}) collective-permute-start(f32[1,2,45,4,32]{2,4,3,1,0:T(8,128)S(1)} %get-tuple-element.14), channel_id=1, source_target_pairs={{1,0},{2,1},{3,2},{4,3},{5,4},{6,5},{7,6},{8,7},{9,8},{10,9},{11,1... | collective-permute-start | bytes 138248 | tf_op jit(solution)/shard_map/ppermute | solution.py:21
  74.1 0.9 %copy.79 = f32[2,135,256]{2,0,1:T(2,128)} copy(f32[2,135,256]{1,2,0:T(8,128)S(1)} %bitcast.144) | data formatting | bytes 552960
  75.4 0.9 %collective-permute-done.4 = f32[1,2,45,4,32]{2,4,3,1,0:T(8,128)S(1)} collective-permute-done((f32[1,2,45,4,32]{2,4,3,1,0:T(8,128)}, f32[1,2,45,4,32]{2,4,3,1,0:T(8,128)S(1)}, u32[]{:S(2)}, u32[]{:S(2)}) %collective-permute-start.4) | collective-permute-done | bytes 46112 | tf_op jit(solution)/shard_map/ppermute | solution.py:18
  76.3 5.7 %collective-permute-done.5 = f32[1,2,45,4,32]{2,4,3,1,0:T(8,128)S(1)} collective-permute-done((f32[1,2,45,4,32]{2,4,3,1,0:T(8,128)S(1)}, f32[1,2,45,4,32]{2,4,3,1,0:T(8,128)S(1)}, u32[]{:S(2)}, u32[]{:S(2)}) %collective-permute-start.5) | collective-permute-done | bytes 46112 | tf_op jit(solution)/shard_map/ppermute | solution.py:21
  82.8 0.7 scatter_fusion.2
  85.0 1.0 %copy.80 = f32[2,45,768]{2,0,1:T(2,128)} copy(f32[2,45,768]{1,2,0:T(8,128)S(1)} %bitcast.143) | data formatting | bytes 552960
  (87 shorter events, 12.7 us)
Async XLA Ops:
  4.1 23.7 %copy-start.9 = (f32[2,135,270]{2,0,1:T(2,128)S(1)}, f32[2,135,270]{2,0,1:T(2,128)}, u32[]{:S(2)}) copy-start(f32[2,135,270]{2,0,1:T(2,128)} %param.14) | copy-start | bytes 874804
  5.0 31.8 %collective-permute-start = (f32[1,2,45,4,32]{2,4,3,1,0:T(8,128)}, f32[1,2,45,4,32]{2,4,3,1,0:T(8,128)}, u32[]{:S(2)}, u32[]{:S(2)}) collective-permute-start(f32[1,2,45,4,32]{2,4,3,1,0:T(8,128)} %get-tuple-element.21), channel_id=1, source_target_pairs={{0,1},{1,2},{2,3},{3,4},{4,5},{5,6},{6,7},{7,8},{8,9},{9,10},{10,1... | collective-permute-start | bytes 138248 | tf_op jit(solution)/shard_map/ppermute | solution.py:18
  7.9 29.8 %collective-permute-start.1 = (f32[1,2,45,4,32]{2,4,3,1,0:T(8,128)}, f32[1,2,45,4,32]{2,4,3,1,0:T(8,128)}, u32[]{:S(2)}, u32[]{:S(2)}) collective-permute-start(f32[1,2,45,4,32]{2,4,3,1,0:T(8,128)} %get-tuple-element.20), channel_id=1, source_target_pairs={{1,0},{2,1},{3,2},{4,3},{5,4},{6,5},{7,6},{8,7},{9,8},{10,9},{11,1... | collective-permute-start | bytes 138248 | tf_op jit(solution)/shard_map/ppermute | solution.py:21
  10.8 27.8 %collective-permute-start.2 = (f32[1,2,45,4,32]{2,4,3,1,0:T(8,128)}, f32[1,2,45,4,32]{2,4,3,1,0:T(8,128)}, u32[]{:S(2)}, u32[]{:S(2)}) collective-permute-start(f32[1,2,45,4,32]{2,4,3,1,0:T(8,128)} %get-tuple-element.19), channel_id=1, source_target_pairs={{0,24},{24,48},{48,72},{72,96},{96,120},{120,144},{144,168},{168,1... | collective-permute-start | bytes 138248 | tf_op jit(solution)/shard_map/ppermute | solution.py:18
  12.8 26.9 %collective-permute-start.3 = (f32[1,2,45,4,32]{2,4,3,1,0:T(8,128)}, f32[1,2,45,4,32]{2,4,3,1,0:T(8,128)}, u32[]{:S(2)}, u32[]{:S(2)}) collective-permute-start(f32[1,2,45,4,32]{2,4,3,1,0:T(8,128)} %get-tuple-element.18), channel_id=1, source_target_pairs={{24,0},{48,24},{72,48},{96,72},{120,96},{144,120},{168,144},{192,1... | collective-permute-start | bytes 138248 | tf_op jit(solution)/shard_map/ppermute | solution.py:21
  27.7 2.0 %copy-start.11 = (f32[2,135,135]{2,0,1:T(2,128)S(1)}, f32[2,135,135]{2,0,1:T(2,128)}, u32[]{:S(2)}) copy-start(f32[2,135,135]{2,0,1:T(2,128)} %param.13) | copy-start | bytes 437404
  28.2 2.4 %copy-start.7 = (f32[2,270,270]{2,0,1:T(2,128)S(1)}, f32[2,270,270]{2,0,1:T(2,128)}, u32[]{:S(2)}) copy-start(f32[2,270,270]{2,0,1:T(2,128)} %param.16) | copy-start | bytes 1749604
  31.2 1.8 %copy-start.10 = (f32[2,270,135]{1,0,2:T(2,128)S(1)}, f32[2,270,135]{1,0,2:T(2,128)}, u32[]{:S(2)}) copy-start(f32[2,270,135]{1,0,2:T(2,128)} %param.15) | copy-start | bytes 874804
  33.0 2.1 %copy-start.13 = (f32[135,8]{0,1:T(8,128)S(1)}, f32[135,8]{0,1:T(8,128)}, u32[]{:S(2)}) copy-start(f32[135,8]{0,1:T(8,128)} %param.12) | copy-start | bytes 12964
  35.0 1.0 %copy-start.12 = (f32[2,135,256]{2,0,1:T(2,128)S(1)}, f32[2,135,256]{2,0,1:T(2,128)}, u32[]{:S(2)}) copy-start(f32[2,135,256]{2,0,1:T(2,128)} %param.11) | copy-start | bytes 829444
  43.5 2.3 %copy-start.1 = (f32[135,270]{1,0:T(8,128)S(1)}, f32[135,270]{1,0:T(8,128)}, u32[]{:S(2)}) copy-start(f32[135,270]{1,0:T(8,128)} %get-tuple-element.42) | copy-start | bytes 437404
  43.5 2.3 %copy-start.2 = (f32[135,270]{1,0:T(8,128)S(1)}, f32[135,270]{1,0:T(8,128)}, u32[]{:S(2)}) copy-start(f32[135,270]{1,0:T(8,128)} %get-tuple-element.43) | copy-start | bytes 437404
  43.5 2.3 %copy-start.5 = (f32[135,270]{1,0:T(8,128)S(1)}, f32[135,270]{1,0:T(8,128)}, u32[]{:S(2)}) copy-start(f32[135,270]{1,0:T(8,128)} %fusion.41) | copy-start | bytes 437404
  45.9 1.1 %copy-start = (f32[2,135,270,1]{2,1,0,3:T(8,128)S(1)}, f32[2,135,270,1]{2,1,0,3:T(8,128)}, u32[]{:S(2)}) copy-start(f32[2,135,270,1]{2,1,0,3:T(8,128)} %reshape.396) | copy-start | bytes 874804
  47.0 1.9 %copy-start.8 = (f32[270,270]{1,0:T(8,128)S(1)}, f32[270,270]{1,0:T(8,128)}, u32[]{:S(2)}) copy-start(f32[270,270]{1,0:T(8,128)} %get-tuple-element.46) | copy-start | bytes 874804
  48.9 2.9 %copy-start.3 = (f32[270,135]{0,1:T(8,128)S(1)}, f32[270,135]{0,1:T(8,128)}, u32[]{:S(2)}) copy-start(f32[270,135]{0,1:T(8,128)} %get-tuple-element.48) | copy-start | bytes 437404
  48.9 2.9 %copy-start.4 = (f32[270,135]{0,1:T(8,128)S(1)}, f32[270,135]{0,1:T(8,128)}, u32[]{:S(2)}) copy-start(f32[270,135]{0,1:T(8,128)} %get-tuple-element.49) | copy-start | bytes 437404
  48.9 2.9 %copy-start.6 = (f32[270,135]{0,1:T(8,128)S(1)}, f32[270,135]{0,1:T(8,128)}, u32[]{:S(2)}) copy-start(f32[270,135]{0,1:T(8,128)} %fusion.42) | copy-start | bytes 437404
  59.5 14.5 %copy-start.14 = (s32[1,1,4,4]{3,2,1,0:T(4,128)S(1)}, s32[1,1,4,4]{3,2,1,0:T(4,128)}, u32[]{:S(2)}) copy-start(s32[1,1,4,4]{3,2,1,0:T(4,128)} %param.18) | copy-start | bytes 196
  60.4 14.7 %collective-permute-start.7 = (f32[1,2,45,4,32]{2,4,3,1,0:T(8,128)S(1)}, f32[1,2,45,4,32]{2,4,3,1,0:T(8,128)S(1)}, u32[]{:S(2)}, u32[]{:S(2)}) collective-permute-start(f32[1,2,45,4,32]{2,4,3,1,0:T(8,128)S(1)} %maximum_bitcast_fusion.1), channel_id=1, source_target_pairs={{24,0},{48,24},{72,48},{96,72},{120,96},{144,120},{168,144},{192,1... | collective-permute-start | bytes 138248 | tf_op jit(solution)/shard_map/ppermute | solution.py:21
  63.2 12.1 %collective-permute-start.6 = (f32[1,2,45,4,32]{2,4,3,1,0:T(8,128)S(1)}, f32[1,2,45,4,32]{2,4,3,1,0:T(8,128)S(1)}, u32[]{:S(2)}, u32[]{:S(2)}) collective-permute-start(f32[1,2,45,4,32]{2,4,3,1,0:T(8,128)S(1)} %maximum_bitcast_fusion), channel_id=1, source_target_pairs={{0,24},{24,48},{48,72},{72,96},{96,120},{120,144},{144,168},{168,1... | collective-permute-start | bytes 138248 | tf_op jit(solution)/shard_map/ppermute | solution.py:18
  65.2 11.1 %collective-permute-start.4 = (f32[1,2,45,4,32]{2,4,3,1,0:T(8,128)}, f32[1,2,45,4,32]{2,4,3,1,0:T(8,128)S(1)}, u32[]{:S(2)}, u32[]{:S(2)}) collective-permute-start(f32[1,2,45,4,32]{2,4,3,1,0:T(8,128)} %get-tuple-element.15), channel_id=1, source_target_pairs={{0,1},{1,2},{2,3},{3,4},{4,5},{5,6},{6,7},{7,8},{8,9},{9,10},{10,1... | collective-permute-start | bytes 138248 | tf_op jit(solution)/shard_map/ppermute | solution.py:18
  72.1 9.9 %collective-permute-start.5 = (f32[1,2,45,4,32]{2,4,3,1,0:T(8,128)S(1)}, f32[1,2,45,4,32]{2,4,3,1,0:T(8,128)S(1)}, u32[]{:S(2)}, u32[]{:S(2)}) collective-permute-start(f32[1,2,45,4,32]{2,4,3,1,0:T(8,128)S(1)} %get-tuple-element.14), channel_id=1, source_target_pairs={{1,0},{2,1},{3,2},{4,3},{5,4},{6,5},{7,6},{8,7},{9,8},{10,9},{11,1... | collective-permute-start | bytes 138248 | tf_op jit(solution)/shard_map/ppermute | solution.py:21
where the time goes:
time: 86.6 us; the launch traced here: 86 us
  starting transfers between devices  36.3 us (42%)
  local copies, waits for them, and re-layouts  21.5 us (25%)
  other arithmetic  12.7 us (15%)
  waiting for transfers between devices  6.93 us (8%)
  matrix products  6.63 us (8%)
  between operations  1.93 us (2%)
    ppermute x4, starting transfers between devices, padded(): lax.ppermute(lax.slice_in_dim(block, 0, width, axis=dim), axis, backward)  22.6 us
    ppermute x4, starting transfers between devices, padded(): lax.ppermute(lax.slice_in_dim(block, block.shape[dim] - width, None, axis...  13.6 us
    dot_general x4, matrix products, exact_dot(): jnp.dot(left, right, precision=lax.Precision.HIGHEST, preferred_element_t...  6.63 us
    ppermute x4, waiting for transfers between devices, padded(): lax.ppermute(lax.slice_in_dim(block, 0, width, axis=dim), axis, backward)  5.7 us
    unnamed x36, local copies, waits for them, and re-layouts  3.91 us
    scatter-add x1, other arithmetic, element_terms(): jnp.zeros(face_table.shape, jnp.float32).at[:, :, face_index, :]  3.55 us
    gather x2, local copies, waits for them, and re-layouts, element_terms(): gathered = face_table[:, :, face_index, :]  2.9 us
    squeeze x4, local copies, waits for them, and re-layouts, complex_block(): top = jnp.concatenate([matrix[0], -matrix[1]], axis=1)  2.62 us
  transfers between devices with their start and end apart: 8, of which 3 were waited for; matrix products, arithmetic and copies ran while one was open for 14% of the time, Pallas kernels for 0%

commit v1 on v0

v1 whole, which is shorter than its diff:
```python
import math

import jax
import jax.numpy as jnp
from jax import lax
from jax.experimental import pallas as pl
from jax.experimental.pallas import tpu as pltpu
from jax.sharding import PartitionSpec as P

ANG = 32
FD = 45
CD = 135
TILE = 128
F32 = jnp.float32
BF16 = jnp.bfloat16

VM = pl.BlockSpec(memory_space=pltpu.VMEM)
SM = pl.BlockSpec(memory_space=pltpu.SMEM)
HB = pl.BlockSpec(memory_space=pltpu.HBM)


def place():
    s, c = lax.axis_index("span"), lax.axis_index("chord")
    return s, c, lax.axis_size("span")


def sides(s, c):
    odd_s, odd_c = s & 1, c & 1
    return 3 - odd_s, 2 + odd_s, 1 - odd_c, odd_c


def lane_group(rows):
    return lax.broadcasted_iota(jnp.int32, (rows, TILE), 1) >> 5


def shifted(block, source, target):
    return pltpu.roll(block, ((target - source) & 3) * ANG, 1)


def split(x):
    high = x.astype(BF16)
    return high, (x - high.astype(F32)).astype(BF16)


def mm(left, right):
    return jnp.dot(left, right, preferred_element_type=F32)


def triple(left, right):
    (lh, ll), (rh, rl) = left, right
    return mm(lh, rh) + (mm(lh, rl) + mm(ll, rh))


def complex_parts(real_rows, imag_rows):
    re = real_rows[:, :TILE] - imag_rows[:, TILE:]
    im = imag_rows[:, :TILE] + real_rows[:, TILE:]
    return re, im


def rows_of(ref, tile, part, tiles, count):
    return ref.reshape(count * tiles * 2, TILE), pl.ds(2 * tile + part, count, stride=2 * tiles)


def element_columns(first, faces, read, cols, src, scales, alive, ops, field, terms):
    half = first // 4
    group = lane_group(FD)
    for m in range(6):
        refs = [faces[first + k, m] for k in range(4)]
        for part in range(2):
            value = None
            for k, ref in enumerate(refs):
                moved = shifted(read(ref >> 2, part), ref & 3, k)
                value = moved if k == 0 else jnp.where(group == k, moved, value)
            cols[pl.ds(FD * m, FD), pl.ds(TILE * part, TILE)] = value
    x = split(cols[...])
    lh, ll, ih, il, th, tl, sh, sl = ops
    re, im = complex_parts(*[triple((lh[p], ll[p]), x) for p in range(2)])
    scale = scales[:, pl.ds(TILE * half, TILE)]
    rhs = split(jnp.concatenate([scale * (src[0, half] - re), scale * (src[1, half] - im)], axis=1))
    re, im = complex_parts(*[triple((ih[p], il[p]), rhs) for p in range(2)])
    alive = alive[:, pl.ds(TILE * half, TILE)]
    re, im = re * alive, im * alive
    field[0], field[1] = re, im
    inner = split(jnp.concatenate([re, im], axis=1))
    out = [triple((th[p], tl[p]), inner) + triple((sh[p], sl[p]), x) for p in range(2)]
    for part, value in enumerate(complex_parts(*out)):
        value = value * alive
        for m in range(6):
            terms[m, part] = value[FD * m : FD * m + FD]


def turn(re, im, sign, angles):
    cosine = jnp.where(sign == 0, 1.0, angles[0:1, :])
    sine = sign.astype(F32) * angles[1:2, :]
    return re * cosine - im * sine, re * sine + im * cosine


def pack_kernel(send_far, traces, on_chip, span, even, odd, near, send_near, send, sems):
    s, c, _ = place()
    group = lane_group(FD)
    numbers = pltpu.make_async_copy(send_far, send, sems.at[0])
    values = pltpu.make_async_copy(traces, near, sems.at[1])
    keep = pltpu.make_async_copy(send_far, send_near, sems.at[2])
    numbers.start()
    values.start()
    keep.start()
    numbers.wait()
    values.wait()
    keep.wait()
    for side, out in zip(sides(s, c), (on_chip, span, even, odd)):
        faces = [send[0, 0, side, j] for j in range(4)]
        for part in range(2):
            value = None
            for j, face in enumerate(faces):
                flat, rows = rows_of(near, face >> 2, part, 6, FD)
                moved = shifted(flat[rows, :], face & 3, j)
                value = moved if j == 0 else jnp.where(group == j, moved, value)
            out[part] = value


def prepare_kernel(lift, inv, trace, stab, source, numbers, total, scales, *rest):
    outs, (src, wide, angles, faces, alive) = rest[:8], rest[8:13]
    held, plain, sems = rest[13:18], rest[18], rest[19]
    copies = [
        pltpu.make_async_copy(ref, slot, sems.at[k])
        for k, (ref, slot) in enumerate(zip((lift, inv, trace, stab, source), held))
    ]
    copies.append(pltpu.make_async_copy(numbers, faces, sems.at[5]))
    for copy in copies:
        copy.start()
    turns = lax.broadcasted_iota(jnp.int32, (1, TILE), 1) & (ANG - 1)
    sigma = 2.0 * math.pi * turns.astype(F32) / ANG
    angles[0:1, :], angles[1:2, :] = jnp.cos(sigma), jnp.sin(sigma)
    column = lax.broadcasted_iota(jnp.int32, (CD, 2 * TILE), 1) >> 5
    tall = scales[...].T
    value = None
    for e in range(8):
        spread = jnp.broadcast_to(tall[:, e : e + 1], (CD, 2 * TILE))
        value = spread if e == 0 else jnp.where(column == e, spread, value)
    wide[...] = value
    for k, (copy, slot) in enumerate(zip(copies[:4], held)):
        copy.wait()
        for part in range(2):
            rows, _, columns = slot.shape
            plain[pl.ds(0, rows), pl.ds(0, columns)] = slot[:, part, :]
            matrix = plain[pl.ds(0, rows), pl.ds(0, columns)]
            if k == 2:
                matrix = matrix.T
            outs[2 * k][part], outs[2 * k + 1][part] = split(matrix)
    copies[4].wait()
    for part in range(2):
        for half in range(2):
            flat, rows = rows_of(held[4], half, part, 2, CD)
            src[part, half] = flat[rows, :]
    copies[5].wait()
    element = lax.broadcasted_iota(jnp.int32, (1, 2 * TILE), 1) >> 5
    alive[...] = (element < total[...]).astype(F32)


def edge_kernel(faces, traces, span, odd, even, on_chip, src, scales, alive, angles, *rest):
    ops, (b_on, b_span, b_even, b_odd, field, terms, table, cols, where) = rest[:8], rest[8:]
    s, c, length = place()
    side = sides(s, c)
    sign = jnp.where(s == 0, -1, jnp.where(s == length - 1, 1, 0))
    for tile in range(6):
        for part in range(2):
            flat, rows = rows_of(traces, tile, part, 6, FD)
            table[tile, part] = flat[rows, :]
    for d, ref in zip((side[0], side[2], side[3]), (on_chip, even, odd)):
        for part in range(2):
            table[6 + d, part] = ref[part]
    table[6 + side[1], 0], table[6 + side[1], 1] = turn(span[0], span[1], sign, angles)
    for k in range(4):
        for m in range(6):
            where[faces[k, m]] = 4 * m + k
    element_columns(
        0, faces, lambda tile, part: table[tile, part], cols, src, scales, alive, ops, field, terms
    )
    group = lane_group(FD)
    for d, ref in zip(side, (b_on, b_span, b_even, b_odd)):
        spots = [where[24 + 4 * d + j] for j in range(4)]
        parts = []
        for part in range(2):
            value = None
            for j, spot in enumerate(spots):
                moved = shifted(terms[spot >> 2, part], spot & 3, j)
                value = moved if j == 0 else jnp.where(group == j, moved, value)
            parts.append(value)
        if ref is b_span:
            parts = turn(*parts, -sign, angles)
        ref[0], ref[1] = parts


def inner_kernel(faces, traces, src, scales, alive, edge_field, edge_terms, *rest):
    ops, (field, sums, cols, inner, terms) = rest[:8], rest[8:]

    def read(tile, part):
        flat, rows = rows_of(traces, tile, part, 6, FD)
        return flat[rows, :]

    element_columns(4, faces, read, cols, src, scales, alive, ops, inner, terms)
    for part in range(2):
        for half, values in enumerate((edge_field, inner)):
            flat, rows = rows_of(field, half, part, 2, CD)
            flat[rows, :] = values[part]
    sums[...] = jnp.zeros(sums.shape, F32)
    group = lane_group(FD)
    for source, first in ((edge_terms, 0), (terms, 4)):
        for m in range(6):
            for k in range(4):
                ref = faces[first + k, m]
                hit = group == (ref & 3)
                for part in range(2):
                    sums[ref >> 2, part] += jnp.where(hit, shifted(source[m, part], k, ref & 3), 0.0)


def final_kernel(send, total, span, even, odd, on_chip, out, sums):
    s, c, _ = place()
    sums[...] = total[pl.ds(0, 6)]
    group = lane_group(FD)
    for side, ref in zip(sides(s, c), (on_chip, span, even, odd)):
        for j in range(4):
            face = send[0, 0, side, j]
            hit = group == (face & 3)
            for part in range(2):
                sums[face >> 2, part] += jnp.where(hit, shifted(ref[part], j, face & 3), 0.0)
    for tile in range(6):
        for part in range(2):
            flat, rows = rows_of(out, tile, part, 6, FD)
            flat[rows, :] = sums[tile, part]


def swaps(count, periodic):
    even = [(i, i ^ 1) for i in range(count)]
    odd = [pair for i in range(1, count - 1, 2) for pair in ((i, i + 1), (i + 1, i))]
    if periodic:
        odd += [(count - 1, 0), (0, count - 1)]
    return even, odd


def exchange(on_chip, span, even, odd, odd_first):
    span_even, span_odd = swaps(lax.axis_size("span"), True)
    chord_even, chord_odd = swaps(lax.axis_size("chord"), False)
    plan = [(even, "chord", chord_even), (odd, "chord", chord_odd)]
    if odd_first:
        plan.reverse()
    plan = [(span, "span", span_odd), *plan, (on_chip, "span", span_even)]
    return [lax.ppermute(*step) for step in plan]


def shape(*dims, dtype=F32):
    return jax.ShapeDtypeStruct(dims, dtype)


def params(**kwargs):
    return pltpu.CompilerParams(vmem_limit_bytes=32 * 1024 * 1024, **kwargs)


def cost(flops, size):
    return pl.CostEstimate(flops=flops, bytes_accessed=size, transcendentals=0)


def interleaved(array):
    _, rows, lanes = array.shape
    return array.transpose(1, 0, 2).reshape(rows, 2, lanes // TILE, TILE).transpose(0, 2, 1, 3)


def hbm(array):
    return pltpu.with_memory_space_constraint(array, pltpu.HBM)


def parted(array):
    rows, tiles = array.shape[:2]
    return array.transpose(0, 2, 1, 3).reshape(rows, 2, tiles * TILE).transpose(1, 0, 2)


def local(
    traces, source, scales, inverse_local, lift_map, trace_map, stabilizer, elem_faces, send_faces, counts
):
    buffers = (shape(2, FD, TILE),) * 4
    linear = shape(FD, 6, 2, TILE)

    *sent, near, send_near = pl.pallas_call(
        pack_kernel,
        out_shape=buffers + (linear, shape(*send_faces.shape, dtype=jnp.int32)),
        in_specs=[HB, HB],
        out_specs=[VM] * 6,
        scratch_shapes=[pltpu.SMEM((1, 1, 4, 4), jnp.int32), pltpu.SemaphoreType.DMA((3,))],
        compiler_params=params(),
        cost_estimate=cost(0, 600_000),
        name="pack",
    )(hbm(send_faces), hbm(interleaved(traces)))
    ghosts = exchange(*sent, True)
    weights = (
        lift_map.transpose(1, 0, 2),
        inverse_local.transpose(1, 0, 2),
        trace_map.transpose(2, 0, 1),
        stabilizer.transpose(1, 0, 2),
    )
    wide_source = interleaved(source)
    *ops, src, wide, angles, faces, alive = pl.pallas_call(
        prepare_kernel,
        out_shape=[
            shape(*w.shape, dtype=BF16)
            for w in (lift_map, inverse_local, trace_map, stabilizer)
            for _ in range(2)
        ]
        + [shape(2, 2, CD, TILE), shape(CD, 2 * TILE), shape(2, TILE)]
        + [shape(*elem_faces.shape, dtype=jnp.int32), shape(1, 2 * TILE)],
        in_specs=[HB] * 6 + [VM] * 2,
        out_specs=[VM] * 13,
        scratch_shapes=[pltpu.VMEM(w.shape, F32) for w in weights + (wide_source,)]
        + [
            pltpu.VMEM(weights[3].shape[::2], F32),
            pltpu.SemaphoreType.DMA((6,)),
        ],
        compiler_params=params(),
        cost_estimate=cost(0, 3_000_000),
        name="prepare",
    )(*map(hbm, weights), hbm(wide_source), hbm(elem_faces), counts, scales.T)
    *back, edge_field, edge_terms = pl.pallas_call(
        edge_kernel,
        out_shape=buffers + (shape(2, CD, TILE), shape(6, 2, FD, TILE)),
        in_specs=[SM] + [VM] * 17,
        out_specs=[VM] * 6,
        scratch_shapes=[
            pltpu.VMEM((10, 2, FD, TILE), F32),
            pltpu.VMEM((6 * FD, 2 * TILE), F32),
            pltpu.SMEM((40,), jnp.int32),
        ],
        compiler_params=params(),
        cost_estimate=cost(1_000_000_000, 3_000_000),
        name="edge_elements",
    )(faces, near, *ghosts, src, wide, alive, angles, *ops)
    returned = exchange(*back, False)
    field, total = pl.pallas_call(
        inner_kernel,
        out_shape=(shape(CD, 2, 2, TILE), shape(10, 2, FD, TILE)),
        in_specs=[SM] + [VM] * 14,
        out_specs=[VM] * 2,
        scratch_shapes=[
            pltpu.VMEM((6 * FD, 2 * TILE), F32),
            pltpu.VMEM((2, CD, TILE), F32),
            pltpu.VMEM((6, 2, FD, TILE), F32),
        ],
        compiler_params=params(),
        cost_estimate=cost(1_000_000_000, 3_000_000),
        name="inner_elements",
    )(faces, near, src, wide, alive, edge_field, edge_terms, *ops)
    residual = pl.pallas_call(
        final_kernel,
        out_shape=linear,
        in_specs=[SM] + [VM] * 5,
        out_specs=VM,
        scratch_shapes=[pltpu.VMEM((6, 2, FD, TILE), F32)],
        compiler_params=params(),
        cost_estimate=cost(0, 1_000_000),
        name="final_sum",
    )(send_near, total, *returned)
    return parted(field), parted(residual)


def solution(mesh):
    spread = ("span", "chord")
    in_specs = (
        P(None, None, spread),
        P(None, None, spread),
        P(None, spread),
        P(),
        P(),
        P(),
        P(),
        P(spread, None),
        P("span", "chord", None, None),
        P("span", "chord"),
    )
    out_specs = (P(None, None, spread), P(None, None, spread))
    return jax.shard_map(local, mesh=mesh, in_specs=in_specs, out_specs=out_specs, check_vma=False)
```

time: 86.6 us -> 51.4 us (0.59)
  the two profiles are of different devices: /device:TPU:152 before, /device:TPU:33 now
where the time goes in v1:
time: 51.4 us; the launch traced here: 51.1 us
  starting transfers between devices  38.5 us (75%)
  Pallas kernels  11.1 us (22%)
  between operations  1.42 us (3%)
    ppermute x8, starting transfers between devices, exchange(): return [lax.ppermute(*step) for step in plan]  38.5 us
    pallas_call x1, Pallas kernels, local(): pl.pallas_call(inner_kernel, out_shape=(shape(CD, 2, 2, TILE), shape(10,...  3.35 us
    pallas_call x1, Pallas kernels, local(): pl.pallas_call(edge_kernel, out_shape=buffers + (shape(2, CD, TILE), shap...  2.68 us
    pallas_call x1, Pallas kernels, local(): pl.pallas_call(prepare_kernel, out_shape=[shape(*w.shape, dtype=BF16) for...  2.21 us
    pallas_call x1, Pallas kernels, local(): pl.pallas_call(final_kernel, out_shape=linear, in_specs=[SM] + [VM] * 5,...  1.58 us
    pallas_call x1, Pallas kernels, local(): pl.pallas_call(pack_kernel, out_shape=buffers + (linear, shape(*send_face...  1.26 us
  transfers between devices with their start and end apart: 8, of which 0 were waited for; matrix products, arithmetic and copies ran while one was open for 0% of the time, Pallas kernels for 11%

profile of v1, /device:TPU:33, one launch (start us, length us, event | category | flops | bytes accessed | tf_op | source)
XLA Modules:
  0.0 51.1 jit_solution(14479666083998154560)
XLA Ops:
  0.6 1.3 %pack.1 = (f32[2,45,128]{2,1,0:T(8,128)S(1)}, f32[2,45,128]{2,1,0:T(8,128)S(1)}, f32[2,45,128]{2,1,0:T(8,128)S(1)}, f32[2,45,128]{2,1,0:T(8,128)S(1)}, f32[45,6,...) custom-call(s32[1,1,4,4]{3,2,1,0:T(4,128)} %send_far.1, f32[45,6,2,128]{3,2,1,0:T(2,128)} %bitcast.29), custom_call_target="tpu_custom_call" | custom-call | bytes 600000 | tf_op jit(solution)/shard_map/pack/pallas_call | solution.py:283
  1.9 8.2 %collective-permute-start = (f32[2,45,128]{2,1,0:T(8,128)S(1)}, f32[2,45,128]{2,1,0:T(8,128)S(1)}, u32[]{:S(2)}, u32[]{:S(2)}) collective-permute-start(f32[2,45,128]{2,1,0:T(8,128)S(1)} %get-tuple-element.34), channel_id=1, source_target_pairs={{24,48},{48,24},{72,96},{96,72},{120,144},{144,120},{168,192},{192... | collective-permute-start | bytes 138248 | tf_op jit(solution)/shard_map/ppermute | solution.py:248
  10.1 6.9 %collective-permute-start.1 = (f32[2,45,128]{2,1,0:T(8,128)S(1)}, f32[2,45,128]{2,1,0:T(8,128)S(1)}, u32[]{:S(2)}, u32[]{:S(2)}) collective-permute-start(f32[2,45,128]{2,1,0:T(8,128)S(1)} %get-tuple-element.35), channel_id=1, source_target_pairs={{1,2},{2,1},{3,4},{4,3},{5,6},{6,5},{7,8},{8,7},{9,10},{10,9},{11,... | collective-permute-start | bytes 138248 | tf_op jit(solution)/shard_map/ppermute | solution.py:248
  17.0 0.0 copy-start
  17.0 2.3 %collective-permute-start.2 = (f32[2,45,128]{2,1,0:T(8,128)S(1)}, f32[2,45,128]{2,1,0:T(8,128)S(1)}, u32[]{:S(2)}, u32[]{:S(2)}) collective-permute-start(f32[2,45,128]{2,1,0:T(8,128)S(1)} %get-tuple-element.36), channel_id=1, source_target_pairs={{0,1},{1,0},{2,3},{3,2},{4,5},{5,4},{6,7},{7,6},{8,9},{9,8},{10,11... | collective-permute-start | bytes 138248 | tf_op jit(solution)/shard_map/ppermute | solution.py:248
  19.3 8.2 %collective-permute-start.3 = (f32[2,45,128]{2,1,0:T(8,128)S(1)}, f32[2,45,128]{2,1,0:T(8,128)S(1)}, u32[]{:S(2)}, u32[]{:S(2)}) collective-permute-start(f32[2,45,128]{2,1,0:T(8,128)S(1)} %get-tuple-element.37), channel_id=1, source_target_pairs={{0,24},{24,0},{48,72},{72,48},{96,120},{120,96},{144,168},{168,144... | collective-permute-start | bytes 138248 | tf_op jit(solution)/shard_map/ppermute | solution.py:248
  28.1 0.0 copy-done
  28.1 2.2 %prepare.1 = (bf16[2,135,270]{2,1,0:T(8,128)(2,1)S(1)}, bf16[2,135,270]{2,1,0:T(8,128)(2,1)S(1)}, bf16[2,135,135]{2,1,0:T(8,128)(2,1)S(1)}, bf16[2,135,135]{2,1,...) custom-call(f32[135,2,270]{2,1,0:T(2,128)} %bitcast.27, ...), custom_call_target="tpu_custom_call" | custom-call | bytes 3000000 | tf_op jit(solution)/shard_map/prepare/pallas_call | solution.py:301
  30.4 0.0 collective-permute-done.span
  30.4 0.0 collective-permute-done.1.odd
  30.4 0.0 collective-permute-done.2.even
  30.4 0.0 collective-permute-done.3.on_chip
  30.4 2.7 %edge_elements.1 = (f32[2,45,128]{2,1,0:T(8,128)S(1)}, f32[2,45,128]{2,1,0:T(8,128)S(1)}, f32[2,45,128]{2,1,0:T(8,128)S(1)}, f32[2,45,128]{2,1,0:T(8,128)S(1)}, ...) custom-call(s32[8,6]{1,0:T(8,128)S(1)} %get-tuple-element.29.faces, ...), custom_call_target="tpu_custom_call" | custom-call | flops 1000000000 | bytes 3000000 | tf_op jit(solution)/shard_map/edge_elements/pallas_call | solution.py:321
  33.1 1.9 %collective-permute-start.4 = (f32[2,45,128]{2,1,0:T(8,128)S(1)}, f32[2,45,128]{2,1,0:T(8,128)S(1)}, u32[]{:S(2)}, u32[]{:S(2)}) collective-permute-start(f32[2,45,128]{2,1,0:T(8,128)S(1)} %get-tuple-element.52), channel_id=1, source_target_pairs={{24,48},{48,24},{72,96},{96,72},{120,144},{144,120},{168,192},{192... | collective-permute-start | bytes 138248 | tf_op jit(solution)/shard_map/ppermute | solution.py:248
  35.0 3.0 %collective-permute-start.5 = (f32[2,45,128]{2,1,0:T(8,128)S(1)}, f32[2,45,128]{2,1,0:T(8,128)S(1)}, u32[]{:S(2)}, u32[]{:S(2)}) collective-permute-start(f32[2,45,128]{2,1,0:T(8,128)S(1)} %get-tuple-element.53), channel_id=1, source_target_pairs={{0,1},{1,0},{2,3},{3,2},{4,5},{5,4},{6,7},{7,6},{8,9},{9,8},{10,11... | collective-permute-start | bytes 138248 | tf_op jit(solution)/shard_map/ppermute | solution.py:248
  38.0 4.4 %collective-permute-start.6 = (f32[2,45,128]{2,1,0:T(8,128)S(1)}, f32[2,45,128]{2,1,0:T(8,128)S(1)}, u32[]{:S(2)}, u32[]{:S(2)}) collective-permute-start(f32[2,45,128]{2,1,0:T(8,128)S(1)} %get-tuple-element.54), channel_id=1, source_target_pairs={{1,2},{2,1},{3,4},{4,3},{5,6},{6,5},{7,8},{8,7},{9,10},{10,9},{11,... | collective-permute-start | bytes 138248 | tf_op jit(solution)/shard_map/ppermute | solution.py:248
  42.4 3.7 %collective-permute-start.7 = (f32[2,45,128]{2,1,0:T(8,128)S(1)}, f32[2,45,128]{2,1,0:T(8,128)S(1)}, u32[]{:S(2)}, u32[]{:S(2)}) collective-permute-start(f32[2,45,128]{2,1,0:T(8,128)S(1)} %get-tuple-element.55), channel_id=1, source_target_pairs={{0,24},{24,0},{48,72},{72,48},{96,120},{120,96},{144,168},{168,144... | collective-permute-start | bytes 138248 | tf_op jit(solution)/shard_map/ppermute | solution.py:248
  46.1 3.4 %inner_elements.1 = (f32[135,2,2,128]{3,2,1,0:T(2,128)}, f32[10,2,45,128]{3,2,1,0:T(8,128)S(1)}) custom-call(s32[8,6]{1,0:T(8,128)S(1)} %get-tuple-element.29.faces, f32[45,6,2,128]{3,2,1,0:T(2,128)S(1)} %get-tuple-element.30.traces, f32[2,2,135,128]{3,2,1,0:T(8,128)S(1)} %get-tuple-element.31.src, f32[135,256]{1,0:T(8,128)S(1)} %get-tuple-element.32.scales, ...), custom_call_target="tpu_custom_call" | custom-call | flops 1000000000 | bytes 3000000 | tf_op jit(solution)/shard_map/inner_elements/pallas_call | solution.py:336
  49.5 0.0 collective-permute-done.4.span
  49.5 0.0 collective-permute-done.5.even
  49.5 0.0 collective-permute-done.6.odd
  49.5 0.0 collective-permute-done.7.on_chip
  49.5 1.6 %final_sum.1 = f32[45,6,2,128]{3,2,1,0:T(2,128)} custom-call(s32[1,1,4,4]{3,2,1,0:T(4,128)S(1)} %get-tuple-element.50.send, f32[10,2,45,128]{3,2,1,0:T(8,128)S(1)} %get-tuple-element.51.total, f32[2,45,128]{2,1,0:T(8,128)S(1)} %collective-permute-done.4.span, f32[2,45,128]{2,1,0:T(8,128)S(1)} %collective-permute-done.5.even, ...), custom_call_target="tpu_custom_call" | custom-call | bytes 1000000 | tf_op jit(solution)/shard_map/final_sum/pallas_call | solution.py:350
Async XLA Ops:
  1.9 28.5 %collective-permute-start = (f32[2,45,128]{2,1,0:T(8,128)S(1)}, f32[2,45,128]{2,1,0:T(8,128)S(1)}, u32[]{:S(2)}, u32[]{:S(2)}) collective-permute-start(f32[2,45,128]{2,1,0:T(8,128)S(1)} %get-tuple-element.34), channel_id=1, source_target_pairs={{24,48},{48,24},{72,96},{96,72},{120,144},{144,120},{168,192},{192... | collective-permute-start | bytes 138248 | tf_op jit(solution)/shard_map/ppermute | solution.py:248
  10.1 20.3 %collective-permute-start.1 = (f32[2,45,128]{2,1,0:T(8,128)S(1)}, f32[2,45,128]{2,1,0:T(8,128)S(1)}, u32[]{:S(2)}, u32[]{:S(2)}) collective-permute-start(f32[2,45,128]{2,1,0:T(8,128)S(1)} %get-tuple-element.35), channel_id=1, source_target_pairs={{1,2},{2,1},{3,4},{4,3},{5,6},{6,5},{7,8},{8,7},{9,10},{10,9},{11,... | collective-permute-start | bytes 138248 | tf_op jit(solution)/shard_map/ppermute | solution.py:248
  17.0 11.1 %copy-start = (f32[135,8]{0,1:T(8,128)S(1)}, f32[135,8]{0,1:T(8,128)}, u32[]{:S(2)}) copy-start(f32[135,8]{0,1:T(8,128)} %param.12) | copy-start | bytes 12964
  17.0 13.4 %collective-permute-start.2 = (f32[2,45,128]{2,1,0:T(8,128)S(1)}, f32[2,45,128]{2,1,0:T(8,128)S(1)}, u32[]{:S(2)}, u32[]{:S(2)}) collective-permute-start(f32[2,45,128]{2,1,0:T(8,128)S(1)} %get-tuple-element.36), channel_id=1, source_target_pairs={{0,1},{1,0},{2,3},{3,2},{4,5},{5,4},{6,7},{7,6},{8,9},{9,8},{10,11... | collective-permute-start | bytes 138248 | tf_op jit(solution)/shard_map/ppermute | solution.py:248
  19.3 11.1 %collective-permute-start.3 = (f32[2,45,128]{2,1,0:T(8,128)S(1)}, f32[2,45,128]{2,1,0:T(8,128)S(1)}, u32[]{:S(2)}, u32[]{:S(2)}) collective-permute-start(f32[2,45,128]{2,1,0:T(8,128)S(1)} %get-tuple-element.37), channel_id=1, source_target_pairs={{0,24},{24,0},{48,72},{72,48},{96,120},{120,96},{144,168},{168,144... | collective-permute-start | bytes 138248 | tf_op jit(solution)/shard_map/ppermute | solution.py:248
  33.1 16.4 %collective-permute-start.4 = (f32[2,45,128]{2,1,0:T(8,128)S(1)}, f32[2,45,128]{2,1,0:T(8,128)S(1)}, u32[]{:S(2)}, u32[]{:S(2)}) collective-permute-start(f32[2,45,128]{2,1,0:T(8,128)S(1)} %get-tuple-element.52), channel_id=1, source_target_pairs={{24,48},{48,24},{72,96},{96,72},{120,144},{144,120},{168,192},{192... | collective-permute-start | bytes 138248 | tf_op jit(solution)/shard_map/ppermute | solution.py:248
  35.0 14.5 %collective-permute-start.5 = (f32[2,45,128]{2,1,0:T(8,128)S(1)}, f32[2,45,128]{2,1,0:T(8,128)S(1)}, u32[]{:S(2)}, u32[]{:S(2)}) collective-permute-start(f32[2,45,128]{2,1,0:T(8,128)S(1)} %get-tuple-element.53), channel_id=1, source_target_pairs={{0,1},{1,0},{2,3},{3,2},{4,5},{5,4},{6,7},{7,6},{8,9},{9,8},{10,11... | collective-permute-start | bytes 138248 | tf_op jit(solution)/shard_map/ppermute | solution.py:248
  38.0 11.5 %collective-permute-start.6 = (f32[2,45,128]{2,1,0:T(8,128)S(1)}, f32[2,45,128]{2,1,0:T(8,128)S(1)}, u32[]{:S(2)}, u32[]{:S(2)}) collective-permute-start(f32[2,45,128]{2,1,0:T(8,128)S(1)} %get-tuple-element.54), channel_id=1, source_target_pairs={{1,2},{2,1},{3,4},{4,3},{5,6},{6,5},{7,8},{8,7},{9,10},{10,9},{11,... | collective-permute-start | bytes 138248 | tf_op jit(solution)/shard_map/ppermute | solution.py:248
  42.4 7.1 %collective-permute-start.7 = (f32[2,45,128]{2,1,0:T(8,128)S(1)}, f32[2,45,128]{2,1,0:T(8,128)S(1)}, u32[]{:S(2)}, u32[]{:S(2)}) collective-permute-start(f32[2,45,128]{2,1,0:T(8,128)S(1)} %get-tuple-element.55), channel_id=1, source_target_pairs={{0,24},{24,0},{48,72},{72,48},{96,120},{120,96},{144,168},{168,144... | collective-permute-start | bytes 138248 | tf_op jit(solution)/shard_map/ppermute | solution.py:248

commit v2 on v1

--- a/solution.py
+++ b/solution.py
@@ -8,6 +8,7 @@
 from jax.sharding import PartitionSpec as P
 
 ANG = 32
+EARLY = 0
 FD = 45
 CD = 135
 TILE = 128
@@ -78,7 +79,7 @@
     scale = scales[:, pl.ds(TILE * half, TILE)]
     rhs = split(jnp.concatenate([scale * (src[0, half] - re), scale * (src[1, half] - im)], axis=1))
     re, im = complex_parts(*[triple((ih[p], il[p]), rhs) for p in range(2)])
-    alive = alive[:, pl.ds(TILE * half, TILE)]
+    alive = 1.0 if alive is None else alive[:, pl.ds(TILE * half, TILE)]
     re, im = re * alive, im * alive
     field[0], field[1] = re, im
     inner = split(jnp.concatenate([re, im], axis=1))
@@ -95,66 +96,76 @@
     return re * cosine - im * sine, re * sine + im * cosine
 
 
-def pack_kernel(send_far, traces, on_chip, span, even, odd, near, send_near, send, sems):
+def early(s):
+    return ((s >> 1) & 3) <= EARLY
+
+
+def pack_kernel(send_far, traces, faces_far, *rest):
+    weights, (on_chip, span, even, odd, near, send_near, faces_near) = rest[:6], rest[6:13]
+    ops, (src, wide, angles, field, terms) = rest[13:21], rest[21:26]
+    held, (cols, plain, sems) = rest[26:32], rest[32:]
     s, c, _ = place()
     group = lane_group(FD)
-    numbers = pltpu.make_async_copy(send_far, send, sems.at[0])
-    values = pltpu.make_async_copy(traces, near, sems.at[1])
-    keep = pltpu.make_async_copy(send_far, send_near, sems.at[2])
-    numbers.start()
-    values.start()
-    keep.start()
-    numbers.wait()
-    values.wait()
-    keep.wait()
+    pairs = ((send_far, send_near), (traces, near), (faces_far, faces_near))
+    pairs += tuple(zip(weights, held))
+    copies = [pltpu.make_async_copy(a, b, sems.at[k]) for k, (a, b) in enumerate(pairs)]
+    for copy in copies:
+        copy.start()
+    for copy in copies[:2]:
+        copy.wait()
+
+    def read(tile, part):
+        flat, rows = rows_of(near, tile, part, 6, FD)
+        return flat[rows, :]
+
     for side, out in zip(sides(s, c), (on_chip, span, even, odd)):
-        faces = [send[0, 0, side, j] for j in range(4)]
+        numbers = [send_near[0, 0, side, j] for j in range(4)]
         for part in range(2):
             value = None
-            for j, face in enumerate(faces):
-                flat, rows = rows_of(near, face >> 2, part, 6, FD)
-                moved = shifted(flat[rows, :], face & 3, j)
+            for j, face in enumerate(numbers):
+                moved = shifted(read(face >> 2, part), face & 3, j)
                 value = moved if j == 0 else jnp.where(group == j, moved, value)
             out[part] = value
-
-
-def prepare_kernel(lift, inv, trace, stab, source, numbers, total, scales, *rest):
-    outs, (src, wide, angles, faces, alive) = rest[:8], rest[8:13]
-    held, plain, sems = rest[13:18], rest[18], rest[19]
-    copies = [
-        pltpu.make_async_copy(ref, slot, sems.at[k])
-        for k, (ref, slot) in enumerate(zip((lift, inv, trace, stab, source), held))
-    ]
-    copies.append(pltpu.make_async_copy(numbers, faces, sems.at[5]))
-    for copy in copies:
-        copy.start()
+    for copy in copies[2:]:
+        copy.wait()
+
+    @pl.when(early(s))
+    def _():
+        prepare(held, ops, src, wide, angles, plain)
+        element_columns(4, faces_near, read, cols, src, wide, None, ops, field, terms)
+
+
+def prepare(held, ops, src, wide, angles, plain):
     turns = lax.broadcasted_iota(jnp.int32, (1, TILE), 1) & (ANG - 1)
     sigma = 2.0 * math.pi * turns.astype(F32) / ANG
     angles[0:1, :], angles[1:2, :] = jnp.cos(sigma), jnp.sin(sigma)
+    for k, slot in enumerate(held[:4]):
+        for part in range(2):
+            rows, _, columns = slot.shape
+            plain[pl.ds(0, rows), pl.ds(0, columns)] = slot[:, part, :]
+            matrix = plain[pl.ds(0, rows), pl.ds(0, columns)]
+            if k == 2:
+                matrix = matrix.T
+            ops[2 * k][part], ops[2 * k + 1][part] = split(matrix)
+    for part in range(2):
+        for half in range(2):
+            flat, rows = rows_of(held[4], half, part, 2, CD)
+            src[part, half] = flat[rows, :]
     column = lax.broadcasted_iota(jnp.int32, (CD, 2 * TILE), 1) >> 5
-    tall = scales[...].T
+    tall = held[5][...].T
     value = None
     for e in range(8):
         spread = jnp.broadcast_to(tall[:, e : e + 1], (CD, 2 * TILE))
         value = spread if e == 0 else jnp.where(column == e, spread, value)
     wide[...] = value
-    for k, (copy, slot) in enumerate(zip(copies[:4], held)):
-        copy.wait()
-        for part in range(2):
-            rows, _, columns = slot.shape
-            plain[pl.ds(0, rows), pl.ds(0, columns)] = slot[:, part, :]
-            matrix = plain[pl.ds(0, rows), pl.ds(0, columns)]
-            if k == 2:
-                matrix = matrix.T
-            outs[2 * k][part], outs[2 * k + 1][part] = split(matrix)
-    copies[4].wait()
-    for part in range(2):
-        for half in range(2):
-            flat, rows = rows_of(held[4], half, part, 2, CD)
-            src[part, half] = flat[rows, :]
-    copies[5].wait()
-    element = lax.broadcasted_iota(jnp.int32, (1, 2 * TILE), 1) >> 5
-    alive[...] = (element < total[...]).astype(F32)
+
+
+def prepare_kernel(*refs):
+    held, outs, plain = refs[:6], refs[17:28], refs[28]
+
+    @pl.when(jnp.logical_not(early(place()[0])))
+    def _():
+        prepare(held, outs[:8], *outs[8:], plain)
 
 
 def edge_kernel(faces, traces, span, odd, even, on_chip, src, scales, alive, angles, *rest):
@@ -191,15 +202,28 @@
         ref[0], ref[1] = parts
 
 
-def inner_kernel(faces, traces, src, scales, alive, edge_field, edge_terms, *rest):
+def inner_kernel(faces, traces, src, scales, alive, edge_field, edge_terms, ahead_field, ahead_terms, *rest):
     ops, (field, sums, cols, inner, terms) = rest[:8], rest[8:]
+    ahead = early(place()[0])
 
     def read(tile, part):
         flat, rows = rows_of(traces, tile, part, 6, FD)
         return flat[rows, :]
 
-    element_columns(4, faces, read, cols, src, scales, alive, ops, inner, terms)
+    @pl.when(ahead)
+    def _():
+        inner[...] = ahead_field[...]
+        terms[...] = ahead_terms[...]
+
+    @pl.when(jnp.logical_not(ahead))
+    def _():
+        element_columns(4, faces, read, cols, src, scales, None, ops, inner, terms)
+
+    live = alive[:, pl.ds(TILE, TILE)]
     for part in range(2):
+        inner[part] *= live
+        for m in range(6):
+            terms[m, part] *= live
         for half, values in enumerate((edge_field, inner)):
             flat, rows = rows_of(field, half, part, 2, CD)
             flat[rows, :] = values[part]
@@ -280,44 +304,53 @@
     buffers = (shape(2, FD, TILE),) * 4
     linear = shape(FD, 6, 2, TILE)
 
-    *sent, near, send_near = pl.pallas_call(
-        pack_kernel,
-        out_shape=buffers + (linear, shape(*send_faces.shape, dtype=jnp.int32)),
-        in_specs=[HB, HB],
-        out_specs=[VM] * 6,
-        scratch_shapes=[pltpu.SMEM((1, 1, 4, 4), jnp.int32), pltpu.SemaphoreType.DMA((3,))],
-        compiler_params=params(),
-        cost_estimate=cost(0, 600_000),
-        name="pack",
-    )(hbm(send_faces), hbm(interleaved(traces)))
-    ghosts = exchange(*sent, True)
     weights = (
         lift_map.transpose(1, 0, 2),
         inverse_local.transpose(1, 0, 2),
         trace_map.transpose(2, 0, 1),
         stabilizer.transpose(1, 0, 2),
+        interleaved(source),
+        scales.T,
     )
-    wide_source = interleaved(source)
-    *ops, src, wide, angles, faces, alive = pl.pallas_call(
+    weights = tuple(map(hbm, weights))
+    prepared = [
+        shape(*w.shape, dtype=BF16)
+        for w in (lift_map, inverse_local, trace_map, stabilizer)
+        for _ in range(2)
+    ] + [shape(2, 2, CD, TILE), shape(CD, 2 * TILE), shape(2, TILE)]
+    held = [shape(*w.shape) for w in weights]
+    plain = pltpu.VMEM(weights[3].shape[::2], F32)
+    results = [shape(2, CD, TILE), shape(6, 2, FD, TILE)]
+    numbers = [pltpu.SMEM(a.shape, jnp.int32) for a in (send_faces, elem_faces)]
+    *packed, ahead_field, ahead_terms, k0, k1, k2, k3, k4, k5 = pl.pallas_call(
+        pack_kernel,
+        out_shape=[*buffers, linear, *numbers, *prepared, *results, *held],
+        in_specs=[HB] * 9,
+        out_specs=[VM] * 5 + [SM] * 2 + [VM] * 19,
+        scratch_shapes=[
+            pltpu.VMEM((6 * FD, 2 * TILE), F32),
+            plain,
+            pltpu.SemaphoreType.DMA((9,)),
+        ],
+        compiler_params=params(),
+        cost_estimate=cost(0, 600_000),
+        name="pack",
+    )(hbm(send_faces), hbm(interleaved(traces)), hbm(elem_faces), *weights)
+    sent, near, send_near, faces, ready = packed[:4], packed[4], packed[5], packed[6], packed[7:]
+    ghosts = exchange(*sent, True)
+    ready = pl.pallas_call(
         prepare_kernel,
-        out_shape=[
-            shape(*w.shape, dtype=BF16)
-            for w in (lift_map, inverse_local, trace_map, stabilizer)
-            for _ in range(2)
-        ]
-        + [shape(2, 2, CD, TILE), shape(CD, 2 * TILE), shape(2, TILE)]
-        + [shape(*elem_faces.shape, dtype=jnp.int32), shape(1, 2 * TILE)],
-        in_specs=[HB] * 6 + [VM] * 2,
-        out_specs=[VM] * 13,
-        scratch_shapes=[pltpu.VMEM(w.shape, F32) for w in weights + (wide_source,)]
-        + [
-            pltpu.VMEM(weights[3].shape[::2], F32),
-            pltpu.SemaphoreType.DMA((6,)),
-        ],
+        out_shape=prepared,
+        in_specs=[VM] * 17,
+        out_specs=[VM] * 11,
+        input_output_aliases={6 + k: k for k in range(11)},
+        scratch_shapes=[plain],
         compiler_params=params(),
         cost_estimate=cost(0, 3_000_000),
         name="prepare",
-    )(*map(hbm, weights), hbm(wide_source), hbm(elem_faces), counts, scales.T)
+    )(k0, k1, k2, k3, k4, k5, *ready)
+    ops, (src, wide, angles) = ready[:8], ready[8:]
+    alive = ((jnp.arange(2 * TILE)[None] >> 5) < counts).astype(F32)
     *back, edge_field, edge_terms = pl.pallas_call(
         edge_kernel,
         out_shape=buffers + (shape(2, CD, TILE), shape(6, 2, FD, TILE)),
@@ -336,7 +369,7 @@
     field, total = pl.pallas_call(
         inner_kernel,
         out_shape=(shape(CD, 2, 2, TILE), shape(10, 2, FD, TILE)),
-        in_specs=[SM] + [VM] * 14,
+        in_specs=[SM] + [VM] * 16,
         out_specs=[VM] * 2,
         scratch_shapes=[
             pltpu.VMEM((6 * FD, 2 * TILE), F32),
@@ -346,7 +379,7 @@
         compiler_params=params(),
         cost_estimate=cost(1_000_000_000, 3_000_000),
         name="inner_elements",
-    )(faces, near, src, wide, alive, edge_field, edge_terms, *ops)
+    )(faces, near, src, wide, alive, edge_field, edge_terms, ahead_field, ahead_terms, *ops)
     residual = pl.pallas_call(
         final_kernel,
         out_shape=linear,

time: 51.4 us -> 47.7 us (0.928)
  Pallas kernels: 11.1 us -> 8.49 us
  starting transfers between devices: 38.5 us -> 37.3 us
    pallas_call x1, Pallas kernels: 3.35 us -> 1.41 us  [local(): pl.pallas_call(inner_kernel, out_shape=(shape(CD, 2, 2, TILE), shape(10,...]
    ppermute x8, starting transfers between devices: 38.5 us -> 37.3 us  [exchange(): return [lax.ppermute(*step) for step in plan]]
    pallas_call x1, Pallas kernels: 2.68 us -> 2.06 us  [local(): pl.pallas_call(edge_kernel, out_shape=buffers + (shape(2, CD, TILE), shap...]
    pallas_call x1, Pallas kernels: 1.58 us -> 1.02 us  [local(): pl.pallas_call(final_kernel, out_shape=linear, in_specs=[SM] + [VM] * 5,...]
    pallas_call x2, Pallas kernels: 3.46 us -> 4 us  [the longest x1 3.97 us: local(): pl.pallas_call(pack_kernel, out_shape=[*buffers, linear, *numbers, *prepa...]
  transfers between devices with their start and end apart: 8 -> 8, of which waited for: 0 -> 1; matrix products, arithmetic and copies ran while one was open for 0% -> 0% of each run, Pallas kernels for 11% -> 3%
where the time goes in v2:
time: 47.7 us; the launch traced here: 47.4 us
  starting transfers between devices  37.3 us (78%)
  Pallas kernels  8.49 us (18%)
  between operations  1.41 us (3%)
    ppermute x8, starting transfers between devices, exchange(): return [lax.ppermute(*step) for step in plan]  37.3 us
    pallas_call x1, Pallas kernels, local(): pl.pallas_call(pack_kernel, out_shape=[*buffers, linear, *numbers, *prepa...  3.97 us
    pallas_call x1, Pallas kernels, local(): pl.pallas_call(edge_kernel, out_shape=buffers + (shape(2, CD, TILE), shap...  2.06 us
    pallas_call x1, Pallas kernels, local(): pl.pallas_call(inner_kernel, out_shape=(shape(CD, 2, 2, TILE), shape(10,...  1.41 us
    pallas_call x1, Pallas kernels, local(): pl.pallas_call(final_kernel, out_shape=linear, in_specs=[SM] + [VM] * 5,...  1.02 us
  transfers between devices with their start and end apart: 8, of which 1 were waited for; matrix products, arithmetic and copies ran while one was open for 0% of the time, Pallas kernels for 3%

profile of v2, /device:TPU:33, one launch (start us, length us, event | category | flops | bytes accessed | tf_op | source)
XLA Modules:
  0.0 47.4 jit_solution(15984722984546189058)
XLA Ops:
  0.6 4.0 %pack.1 = (f32[2,45,128]{2,1,0:T(8,128)S(1)}, f32[2,45,128]{2,1,0:T(8,128)S(1)}, f32[2,45,128]{2,1,0:T(8,128)S(1)}, f32[2,45,128]{2,1,0:T(8,128)S(1)}, f32[45,6,...) custom-call(s32[1,1,4,4]{3,2,1,0:T(4,128)} %send_far.1, ...), custom_call_target="tpu_custom_call" | custom-call | bytes 600000 | tf_op jit(solution)/shard_map/pack/pallas_call | solution.py:325
  4.6 5.9 %collective-permute-start = (f32[2,45,128]{2,1,0:T(8,128)S(1)}, f32[2,45,128]{2,1,0:T(8,128)S(1)}, u32[]{:S(2)}, u32[]{:S(2)}) collective-permute-start(f32[2,45,128]{2,1,0:T(8,128)S(1)} %get-tuple-element.68), channel_id=1, source_target_pairs={{24,48},{48,24},{72,96},{96,72},{120,144},{144,120},{168,192},{192... | collective-permute-start | bytes 138248 | tf_op jit(solution)/shard_map/ppermute | solution.py:272
  10.6 6.9 %collective-permute-start.1 = (f32[2,45,128]{2,1,0:T(8,128)S(1)}, f32[2,45,128]{2,1,0:T(8,128)S(1)}, u32[]{:S(2)}, u32[]{:S(2)}) collective-permute-start(f32[2,45,128]{2,1,0:T(8,128)S(1)} %get-tuple-element.69), channel_id=1, source_target_pairs={{1,2},{2,1},{3,4},{4,3},{5,6},{6,5},{7,8},{8,7},{9,10},{10,9},{11,... | collective-permute-start | bytes 138248 | tf_op jit(solution)/shard_map/ppermute | solution.py:272
  17.5 2.3 %collective-permute-start.2 = (f32[2,45,128]{2,1,0:T(8,128)S(1)}, f32[2,45,128]{2,1,0:T(8,128)S(1)}, u32[]{:S(2)}, u32[]{:S(2)}) collective-permute-start(f32[2,45,128]{2,1,0:T(8,128)S(1)} %get-tuple-element.70), channel_id=1, source_target_pairs={{0,1},{1,0},{2,3},{3,2},{4,5},{5,4},{6,7},{7,6},{8,9},{9,8},{10,11... | collective-permute-start | bytes 138248 | tf_op jit(solution)/shard_map/ppermute | solution.py:272
  19.8 8.2 %collective-permute-start.3 = (f32[2,45,128]{2,1,0:T(8,128)S(1)}, f32[2,45,128]{2,1,0:T(8,128)S(1)}, u32[]{:S(2)}, u32[]{:S(2)}) collective-permute-start(f32[2,45,128]{2,1,0:T(8,128)S(1)} %get-tuple-element.71), channel_id=1, source_target_pairs={{0,24},{24,0},{48,72},{72,48},{96,120},{120,96},{144,168},{168,144... | collective-permute-start | bytes 138248 | tf_op jit(solution)/shard_map/ppermute | solution.py:272
  28.7 0.0 collective-permute-done.span
  28.7 0.0 collective-permute-done.1.odd
  28.7 0.0 collective-permute-done.2.even
  28.7 0.1 collective-permute-done.3.on_chip
  28.8 2.1 %edge_elements.1 = (f32[2,45,128]{2,1,0:T(8,128)S(1)}, f32[2,45,128]{2,1,0:T(8,128)S(1)}, f32[2,45,128]{2,1,0:T(8,128)S(1)}, f32[2,45,128]{2,1,0:T(8,128)S(1)}, ...) custom-call(s32[8,6]{1,0:T(8,128)S(4)} %get-tuple-element.47.faces, ...), custom_call_target="tpu_custom_call" | custom-call | flops 1000000000 | bytes 3000000 | tf_op jit(solution)/shard_map/edge_elements/pallas_call | solution.py:354
  30.9 1.9 %collective-permute-start.4 = (f32[2,45,128]{2,1,0:T(8,128)S(1)}, f32[2,45,128]{2,1,0:T(8,128)S(1)}, u32[]{:S(2)}, u32[]{:S(2)}) collective-permute-start(f32[2,45,128]{2,1,0:T(8,128)S(1)} %get-tuple-element.88), channel_id=1, source_target_pairs={{24,48},{48,24},{72,96},{96,72},{120,144},{144,120},{168,192},{192... | collective-permute-start | bytes 138248 | tf_op jit(solution)/shard_map/ppermute | solution.py:272
  32.8 3.9 %collective-permute-start.5 = (f32[2,45,128]{2,1,0:T(8,128)S(1)}, f32[2,45,128]{2,1,0:T(8,128)S(1)}, u32[]{:S(2)}, u32[]{:S(2)}) collective-permute-start(f32[2,45,128]{2,1,0:T(8,128)S(1)} %get-tuple-element.89), channel_id=1, source_target_pairs={{0,1},{1,0},{2,3},{3,2},{4,5},{5,4},{6,7},{7,6},{8,9},{9,8},{10,11... | collective-permute-start | bytes 138248 | tf_op jit(solution)/shard_map/ppermute | solution.py:272
  36.7 3.8 %collective-permute-start.6 = (f32[2,45,128]{2,1,0:T(8,128)S(1)}, f32[2,45,128]{2,1,0:T(8,128)S(1)}, u32[]{:S(2)}, u32[]{:S(2)}) collective-permute-start(f32[2,45,128]{2,1,0:T(8,128)S(1)} %get-tuple-element.90), channel_id=1, source_target_pairs={{1,2},{2,1},{3,4},{4,3},{5,6},{6,5},{7,8},{8,7},{9,10},{10,9},{11,... | collective-permute-start | bytes 138248 | tf_op jit(solution)/shard_map/ppermute | solution.py:272
  40.5 4.5 %collective-permute-start.7 = (f32[2,45,128]{2,1,0:T(8,128)S(1)}, f32[2,45,128]{2,1,0:T(8,128)S(1)}, u32[]{:S(2)}, u32[]{:S(2)}) collective-permute-start(f32[2,45,128]{2,1,0:T(8,128)S(1)} %get-tuple-element.91), channel_id=1, source_target_pairs={{0,24},{24,0},{48,72},{72,48},{96,120},{120,96},{144,168},{168,144... | collective-permute-start | bytes 138248 | tf_op jit(solution)/shard_map/ppermute | solution.py:272
  44.9 1.4 %inner_elements.1 = (f32[135,2,2,128]{3,2,1,0:T(2,128)}, f32[10,2,45,128]{3,2,1,0:T(8,128)S(1)}) custom-call(s32[8,6]{1,0:T(8,128)S(4)} %get-tuple-element.47.faces, f32[45,6,2,128]{3,2,1,0:T(2,128)S(1)} %get-tuple-element.48.traces, f32[2,2,135,128]{3,2,1,0:T(8,128)S(1)} %get-tuple-element.66.src, f32[135,256]{1,0:T(8,128)S(1)} %get-tuple-element.67.scales, ...), custom_call_target="tpu_custom_call" | custom-call | flops 1000000000 | bytes 3000000 | tf_op jit(solution)/shard_map/inner_elements/pallas_call | solution.py:369
  46.3 0.0 collective-permute-done.4.span
  46.4 0.0 collective-permute-done.5.even
  46.4 0.0 collective-permute-done.6.odd
  46.4 0.0 collective-permute-done.7.on_chip
  46.4 1.0 %final_sum.1 = f32[45,6,2,128]{3,2,1,0:T(2,128)} custom-call(s32[1,1,4,4]{3,2,1,0:T(4,128)S(4)} %get-tuple-element.86.send, f32[10,2,45,128]{3,2,1,0:T(8,128)S(1)} %get-tuple-element.87.total, f32[2,45,128]{2,1,0:T(8,128)S(1)} %collective-permute-done.4.span, f32[2,45,128]{2,1,0:T(8,128)S(1)} %collective-permute-done.5.even, ...), custom_call_target="tpu_custom_call" | custom-call | bytes 1000000 | tf_op jit(solution)/shard_map/final_sum/pallas_call | solution.py:383
  (2 shorter events, 0.0 us)
Async XLA Ops:
  4.6 24.0 %collective-permute-start = (f32[2,45,128]{2,1,0:T(8,128)S(1)}, f32[2,45,128]{2,1,0:T(8,128)S(1)}, u32[]{:S(2)}, u32[]{:S(2)}) collective-permute-start(f32[2,45,128]{2,1,0:T(8,128)S(1)} %get-tuple-element.68), channel_id=1, source_target_pairs={{24,48},{48,24},{72,96},{96,72},{120,144},{144,120},{168,192},{192... | collective-permute-start | bytes 138248 | tf_op jit(solution)/shard_map/ppermute | solution.py:272
  10.6 18.1 %collective-permute-start.1 = (f32[2,45,128]{2,1,0:T(8,128)S(1)}, f32[2,45,128]{2,1,0:T(8,128)S(1)}, u32[]{:S(2)}, u32[]{:S(2)}) collective-permute-start(f32[2,45,128]{2,1,0:T(8,128)S(1)} %get-tuple-element.69), channel_id=1, source_target_pairs={{1,2},{2,1},{3,4},{4,3},{5,6},{6,5},{7,8},{8,7},{9,10},{10,9},{11,... | collective-permute-start | bytes 138248 | tf_op jit(solution)/shard_map/ppermute | solution.py:272
  17.5 11.2 %collective-permute-start.2 = (f32[2,45,128]{2,1,0:T(8,128)S(1)}, f32[2,45,128]{2,1,0:T(8,128)S(1)}, u32[]{:S(2)}, u32[]{:S(2)}) collective-permute-start(f32[2,45,128]{2,1,0:T(8,128)S(1)} %get-tuple-element.70), channel_id=1, source_target_pairs={{0,1},{1,0},{2,3},{3,2},{4,5},{5,4},{6,7},{7,6},{8,9},{9,8},{10,11... | collective-permute-start | bytes 138248 | tf_op jit(solution)/shard_map/ppermute | solution.py:272
  19.8 9.0 %collective-permute-start.3 = (f32[2,45,128]{2,1,0:T(8,128)S(1)}, f32[2,45,128]{2,1,0:T(8,128)S(1)}, u32[]{:S(2)}, u32[]{:S(2)}) collective-permute-start(f32[2,45,128]{2,1,0:T(8,128)S(1)} %get-tuple-element.71), channel_id=1, source_target_pairs={{0,24},{24,0},{48,72},{72,48},{96,120},{120,96},{144,168},{168,144... | collective-permute-start | bytes 138248 | tf_op jit(solution)/shard_map/ppermute | solution.py:272
  30.9 15.5 %collective-permute-start.4 = (f32[2,45,128]{2,1,0:T(8,128)S(1)}, f32[2,45,128]{2,1,0:T(8,128)S(1)}, u32[]{:S(2)}, u32[]{:S(2)}) collective-permute-start(f32[2,45,128]{2,1,0:T(8,128)S(1)} %get-tuple-element.88), channel_id=1, source_target_pairs={{24,48},{48,24},{72,96},{96,72},{120,144},{144,120},{168,192},{192... | collective-permute-start | bytes 138248 | tf_op jit(solution)/shard_map/ppermute | solution.py:272
  32.8 13.5 %collective-permute-start.5 = (f32[2,45,128]{2,1,0:T(8,128)S(1)}, f32[2,45,128]{2,1,0:T(8,128)S(1)}, u32[]{:S(2)}, u32[]{:S(2)}) collective-permute-start(f32[2,45,128]{2,1,0:T(8,128)S(1)} %get-tuple-element.89), channel_id=1, source_target_pairs={{0,1},{1,0},{2,3},{3,2},{4,5},{5,4},{6,7},{7,6},{8,9},{9,8},{10,11... | collective-permute-start | bytes 138248 | tf_op jit(solution)/shard_map/ppermute | solution.py:272
  36.7 9.7 %collective-permute-start.6 = (f32[2,45,128]{2,1,0:T(8,128)S(1)}, f32[2,45,128]{2,1,0:T(8,128)S(1)}, u32[]{:S(2)}, u32[]{:S(2)}) collective-permute-start(f32[2,45,128]{2,1,0:T(8,128)S(1)} %get-tuple-element.90), channel_id=1, source_target_pairs={{1,2},{2,1},{3,4},{4,3},{5,6},{6,5},{7,8},{8,7},{9,10},{10,9},{11,... | collective-permute-start | bytes 138248 | tf_op jit(solution)/shard_map/ppermute | solution.py:272
  40.5 5.9 %collective-permute-start.7 = (f32[2,45,128]{2,1,0:T(8,128)S(1)}, f32[2,45,128]{2,1,0:T(8,128)S(1)}, u32[]{:S(2)}, u32[]{:S(2)}) collective-permute-start(f32[2,45,128]{2,1,0:T(8,128)S(1)} %get-tuple-element.91), channel_id=1, source_target_pairs={{0,24},{24,0},{48,72},{72,48},{96,120},{120,96},{144,168},{168,144... | collective-permute-start | bytes 138248 | tf_op jit(solution)/shard_map/ppermute | solution.py:272

commit v3 on v2

--- a/solution.py
+++ b/solution.py
@@ -238,7 +238,7 @@
                     sums[ref >> 2, part] += jnp.where(hit, shifted(source[m, part], k, ref & 3), 0.0)
 
 
-def final_kernel(send, total, span, even, odd, on_chip, out, sums):
+def final_kernel(send, total, span, even, odd, on_chip, out, sums, staged, sems):
     s, c, _ = place()
     sums[...] = total[pl.ds(0, 6)]
     group = lane_group(FD)
@@ -248,10 +248,18 @@
             hit = group == (face & 3)
             for part in range(2):
                 sums[face >> 2, part] += jnp.where(hit, shifted(ref[part], j, face & 3), 0.0)
-    for tile in range(6):
-        for part in range(2):
-            flat, rows = rows_of(out, tile, part, 6, FD)
-            flat[rows, :] = sums[tile, part]
+    copies = []
+    for k, (first, count) in enumerate(((0, 24), (24, FD - 24))):
+        for tile in range(6):
+            for part in range(2):
+                flat = staged.reshape(FD * 12, TILE)
+                rows = pl.ds(12 * first + 2 * tile + part, count, stride=12)
+                flat[rows, :] = sums[tile, part, pl.ds(first, count), :]
+        rows = pl.ds(first, count)
+        copies.append(pltpu.make_async_copy(staged.at[rows], out.at[rows], sems.at[k]))
+        copies[k].start()
+    for copy in copies:
+        copy.wait()
 
 
 def swaps(count, periodic):
@@ -384,8 +392,12 @@
         final_kernel,
         out_shape=linear,
         in_specs=[SM] + [VM] * 5,
-        out_specs=VM,
-        scratch_shapes=[pltpu.VMEM((6, 2, FD, TILE), F32)],
+        out_specs=HB,
+        scratch_shapes=[
+            pltpu.VMEM((6, 2, FD, TILE), F32),
+            pltpu.VMEM((FD, 6, 2, TILE), F32),
+            pltpu.SemaphoreType.DMA((2,)),
+        ],
         compiler_params=params(),
         cost_estimate=cost(0, 1_000_000),
         name="final_sum",

time: 47.7 us -> 47.7 us (level)
  no operation moved by 1% of the time
where the time goes in v3:
time: 47.7 us; the launch traced here: 47.4 us
  starting transfers between devices  37.3 us (78%)
  Pallas kernels  8.49 us (18%)
  between operations  1.41 us (3%)
    ppermute x8, starting transfers between devices, exchange(): return [lax.ppermute(*step) for step in plan]  37.3 us
    pallas_call x1, Pallas kernels, local(): pl.pallas_call(pack_kernel, out_shape=[*buffers, linear, *numbers, *prepa...  3.98 us
    pallas_call x1, Pallas kernels, local(): pl.pallas_call(edge_kernel, out_shape=buffers + (shape(2, CD, TILE), shap...  2.06 us
    pallas_call x1, Pallas kernels, local(): pl.pallas_call(inner_kernel, out_shape=(shape(CD, 2, 2, TILE), shape(10,...  1.42 us
    pallas_call x1, Pallas kernels, local(): pl.pallas_call(final_kernel, out_shape=linear, in_specs=[SM] + [VM] * 5,...  1.02 us
  transfers between devices with their start and end apart: 8, of which 1 were waited for; matrix products, arithmetic and copies ran while one was open for 0% of the time, Pallas kernels for 3%

profile of v3, /device:TPU:33, one launch (start us, length us, event | category | flops | bytes accessed | tf_op | source)
XLA Modules:
  0.0 47.4 jit_solution(13445640770107431134)
XLA Ops:
  0.6 4.0 %pack.1 = (f32[2,45,128]{2,1,0:T(8,128)S(1)}, f32[2,45,128]{2,1,0:T(8,128)S(1)}, f32[2,45,128]{2,1,0:T(8,128)S(1)}, f32[2,45,128]{2,1,0:T(8,128)S(1)}, f32[45,6,...) custom-call(s32[1,1,4,4]{3,2,1,0:T(4,128)} %send_far.1, ...), custom_call_target="tpu_custom_call" | custom-call | bytes 600000 | tf_op jit(solution)/shard_map/pack/pallas_call | solution.py:333
  4.6 5.9 %collective-permute-start = (f32[2,45,128]{2,1,0:T(8,128)S(1)}, f32[2,45,128]{2,1,0:T(8,128)S(1)}, u32[]{:S(2)}, u32[]{:S(2)}) collective-permute-start(f32[2,45,128]{2,1,0:T(8,128)S(1)} %get-tuple-element.68), channel_id=1, source_target_pairs={{24,48},{48,24},{72,96},{96,72},{120,144},{144,120},{168,192},{192... | collective-permute-start | bytes 138248 | tf_op jit(solution)/shard_map/ppermute | solution.py:280
  10.6 6.9 %collective-permute-start.1 = (f32[2,45,128]{2,1,0:T(8,128)S(1)}, f32[2,45,128]{2,1,0:T(8,128)S(1)}, u32[]{:S(2)}, u32[]{:S(2)}) collective-permute-start(f32[2,45,128]{2,1,0:T(8,128)S(1)} %get-tuple-element.69), channel_id=1, source_target_pairs={{1,2},{2,1},{3,4},{4,3},{5,6},{6,5},{7,8},{8,7},{9,10},{10,9},{11,... | collective-permute-start | bytes 138248 | tf_op jit(solution)/shard_map/ppermute | solution.py:280
  17.5 2.3 %collective-permute-start.2 = (f32[2,45,128]{2,1,0:T(8,128)S(1)}, f32[2,45,128]{2,1,0:T(8,128)S(1)}, u32[]{:S(2)}, u32[]{:S(2)}) collective-permute-start(f32[2,45,128]{2,1,0:T(8,128)S(1)} %get-tuple-element.70), channel_id=1, source_target_pairs={{0,1},{1,0},{2,3},{3,2},{4,5},{5,4},{6,7},{7,6},{8,9},{9,8},{10,11... | collective-permute-start | bytes 138248 | tf_op jit(solution)/shard_map/ppermute | solution.py:280
  19.8 8.2 %collective-permute-start.3 = (f32[2,45,128]{2,1,0:T(8,128)S(1)}, f32[2,45,128]{2,1,0:T(8,128)S(1)}, u32[]{:S(2)}, u32[]{:S(2)}) collective-permute-start(f32[2,45,128]{2,1,0:T(8,128)S(1)} %get-tuple-element.71), channel_id=1, source_target_pairs={{0,24},{24,0},{48,72},{72,48},{96,120},{120,96},{144,168},{168,144... | collective-permute-start | bytes 138248 | tf_op jit(solution)/shard_map/ppermute | solution.py:280
  28.7 0.0 collective-permute-done.span
  28.7 0.0 collective-permute-done.1.odd
  28.7 0.0 collective-permute-done.2.even
  28.7 0.1 collective-permute-done.3.on_chip
  28.8 2.1 %edge_elements.1 = (f32[2,45,128]{2,1,0:T(8,128)S(1)}, f32[2,45,128]{2,1,0:T(8,128)S(1)}, f32[2,45,128]{2,1,0:T(8,128)S(1)}, f32[2,45,128]{2,1,0:T(8,128)S(1)}, ...) custom-call(s32[8,6]{1,0:T(8,128)S(4)} %get-tuple-element.47.faces, ...), custom_call_target="tpu_custom_call" | custom-call | flops 1000000000 | bytes 3000000 | tf_op jit(solution)/shard_map/edge_elements/pallas_call | solution.py:362
  30.9 1.9 %collective-permute-start.4 = (f32[2,45,128]{2,1,0:T(8,128)S(1)}, f32[2,45,128]{2,1,0:T(8,128)S(1)}, u32[]{:S(2)}, u32[]{:S(2)}) collective-permute-start(f32[2,45,128]{2,1,0:T(8,128)S(1)} %get-tuple-element.88), channel_id=1, source_target_pairs={{24,48},{48,24},{72,96},{96,72},{120,144},{144,120},{168,192},{192... | collective-permute-start | bytes 138248 | tf_op jit(solution)/shard_map/ppermute | solution.py:280
  32.8 3.9 %collective-permute-start.5 = (f32[2,45,128]{2,1,0:T(8,128)S(1)}, f32[2,45,128]{2,1,0:T(8,128)S(1)}, u32[]{:S(2)}, u32[]{:S(2)}) collective-permute-start(f32[2,45,128]{2,1,0:T(8,128)S(1)} %get-tuple-element.89), channel_id=1, source_target_pairs={{0,1},{1,0},{2,3},{3,2},{4,5},{5,4},{6,7},{7,6},{8,9},{9,8},{10,11... | collective-permute-start | bytes 138248 | tf_op jit(solution)/shard_map/ppermute | solution.py:280
  36.7 3.8 %collective-permute-start.6 = (f32[2,45,128]{2,1,0:T(8,128)S(1)}, f32[2,45,128]{2,1,0:T(8,128)S(1)}, u32[]{:S(2)}, u32[]{:S(2)}) collective-permute-start(f32[2,45,128]{2,1,0:T(8,128)S(1)} %get-tuple-element.90), channel_id=1, source_target_pairs={{1,2},{2,1},{3,4},{4,3},{5,6},{6,5},{7,8},{8,7},{9,10},{10,9},{11,... | collective-permute-start | bytes 138248 | tf_op jit(solution)/shard_map/ppermute | solution.py:280
  40.5 4.4 %collective-permute-start.7 = (f32[2,45,128]{2,1,0:T(8,128)S(1)}, f32[2,45,128]{2,1,0:T(8,128)S(1)}, u32[]{:S(2)}, u32[]{:S(2)}) collective-permute-start(f32[2,45,128]{2,1,0:T(8,128)S(1)} %get-tuple-element.91), channel_id=1, source_target_pairs={{0,24},{24,0},{48,72},{72,48},{96,120},{120,96},{144,168},{168,144... | collective-permute-start | bytes 138248 | tf_op jit(solution)/shard_map/ppermute | solution.py:280
  44.9 1.4 %inner_elements.1 = (f32[135,2,2,128]{3,2,1,0:T(2,128)}, f32[10,2,45,128]{3,2,1,0:T(8,128)S(1)}) custom-call(s32[8,6]{1,0:T(8,128)S(4)} %get-tuple-element.47.faces, f32[45,6,2,128]{3,2,1,0:T(2,128)S(1)} %get-tuple-element.48.traces, f32[2,2,135,128]{3,2,1,0:T(8,128)S(1)} %get-tuple-element.66.src, f32[135,256]{1,0:T(8,128)S(1)} %get-tuple-element.67.scales, ...), custom_call_target="tpu_custom_call" | custom-call | flops 1000000000 | bytes 3000000 | tf_op jit(solution)/shard_map/inner_elements/pallas_call | solution.py:377
  46.3 0.0 collective-permute-done.4.span
  46.3 0.0 collective-permute-done.5.even
  46.3 0.0 collective-permute-done.6.odd
  46.4 0.0 collective-permute-done.7.on_chip
  46.4 1.0 %final_sum.1 = f32[45,6,2,128]{3,2,1,0:T(2,128)} custom-call(s32[1,1,4,4]{3,2,1,0:T(4,128)S(4)} %get-tuple-element.86.send, f32[10,2,45,128]{3,2,1,0:T(8,128)S(1)} %get-tuple-element.87.total, f32[2,45,128]{2,1,0:T(8,128)S(1)} %collective-permute-done.4.span, f32[2,45,128]{2,1,0:T(8,128)S(1)} %collective-permute-done.5.even, ...), custom_call_target="tpu_custom_call" | custom-call | bytes 1000000 | tf_op jit(solution)/shard_map/final_sum/pallas_call | solution.py:391
  (2 shorter events, 0.0 us)
Async XLA Ops:
  4.6 24.0 %collective-permute-start = (f32[2,45,128]{2,1,0:T(8,128)S(1)}, f32[2,45,128]{2,1,0:T(8,128)S(1)}, u32[]{:S(2)}, u32[]{:S(2)}) collective-permute-start(f32[2,45,128]{2,1,0:T(8,128)S(1)} %get-tuple-element.68), channel_id=1, source_target_pairs={{24,48},{48,24},{72,96},{96,72},{120,144},{144,120},{168,192},{192... | collective-permute-start | bytes 138248 | tf_op jit(solution)/shard_map/ppermute | solution.py:280
  10.6 18.1 %collective-permute-start.1 = (f32[2,45,128]{2,1,0:T(8,128)S(1)}, f32[2,45,128]{2,1,0:T(8,128)S(1)}, u32[]{:S(2)}, u32[]{:S(2)}) collective-permute-start(f32[2,45,128]{2,1,0:T(8,128)S(1)} %get-tuple-element.69), channel_id=1, source_target_pairs={{1,2},{2,1},{3,4},{4,3},{5,6},{6,5},{7,8},{8,7},{9,10},{10,9},{11,... | collective-permute-start | bytes 138248 | tf_op jit(solution)/shard_map/ppermute | solution.py:280
  17.5 11.2 %collective-permute-start.2 = (f32[2,45,128]{2,1,0:T(8,128)S(1)}, f32[2,45,128]{2,1,0:T(8,128)S(1)}, u32[]{:S(2)}, u32[]{:S(2)}) collective-permute-start(f32[2,45,128]{2,1,0:T(8,128)S(1)} %get-tuple-element.70), channel_id=1, source_target_pairs={{0,1},{1,0},{2,3},{3,2},{4,5},{5,4},{6,7},{7,6},{8,9},{9,8},{10,11... | collective-permute-start | bytes 138248 | tf_op jit(solution)/shard_map/ppermute | solution.py:280
  19.8 9.0 %collective-permute-start.3 = (f32[2,45,128]{2,1,0:T(8,128)S(1)}, f32[2,45,128]{2,1,0:T(8,128)S(1)}, u32[]{:S(2)}, u32[]{:S(2)}) collective-permute-start(f32[2,45,128]{2,1,0:T(8,128)S(1)} %get-tuple-element.71), channel_id=1, source_target_pairs={{0,24},{24,0},{48,72},{72,48},{96,120},{120,96},{144,168},{168,144... | collective-permute-start | bytes 138248 | tf_op jit(solution)/shard_map/ppermute | solution.py:280
  30.9 15.5 %collective-permute-start.4 = (f32[2,45,128]{2,1,0:T(8,128)S(1)}, f32[2,45,128]{2,1,0:T(8,128)S(1)}, u32[]{:S(2)}, u32[]{:S(2)}) collective-permute-start(f32[2,45,128]{2,1,0:T(8,128)S(1)} %get-tuple-element.88), channel_id=1, source_target_pairs={{24,48},{48,24},{72,96},{96,72},{120,144},{144,120},{168,192},{192... | collective-permute-start | bytes 138248 | tf_op jit(solution)/shard_map/ppermute | solution.py:280
  32.8 13.5 %collective-permute-start.5 = (f32[2,45,128]{2,1,0:T(8,128)S(1)}, f32[2,45,128]{2,1,0:T(8,128)S(1)}, u32[]{:S(2)}, u32[]{:S(2)}) collective-permute-start(f32[2,45,128]{2,1,0:T(8,128)S(1)} %get-tuple-element.89), channel_id=1, source_target_pairs={{0,1},{1,0},{2,3},{3,2},{4,5},{5,4},{6,7},{7,6},{8,9},{9,8},{10,11... | collective-permute-start | bytes 138248 | tf_op jit(solution)/shard_map/ppermute | solution.py:280
  36.7 9.7 %collective-permute-start.6 = (f32[2,45,128]{2,1,0:T(8,128)S(1)}, f32[2,45,128]{2,1,0:T(8,128)S(1)}, u32[]{:S(2)}, u32[]{:S(2)}) collective-permute-start(f32[2,45,128]{2,1,0:T(8,128)S(1)} %get-tuple-element.90), channel_id=1, source_target_pairs={{1,2},{2,1},{3,4},{4,3},{5,6},{6,5},{7,8},{8,7},{9,10},{10,9},{11,... | collective-permute-start | bytes 138248 | tf_op jit(solution)/shard_map/ppermute | solution.py:280
  40.5 5.9 %collective-permute-start.7 = (f32[2,45,128]{2,1,0:T(8,128)S(1)}, f32[2,45,128]{2,1,0:T(8,128)S(1)}, u32[]{:S(2)}, u32[]{:S(2)}) collective-permute-start(f32[2,45,128]{2,1,0:T(8,128)S(1)} %get-tuple-element.91), channel_id=1, source_target_pairs={{0,24},{24,0},{48,72},{72,48},{96,120},{120,96},{144,168},{168,144... | collective-permute-start | bytes 138248 | tf_op jit(solution)/shard_map/ppermute | solution.py:280
